TPU v7x, 128 devices: a whole 4x4x4 slice. The times are simulated.
128 devices in a mesh: dp: 16 (over x, z), tensor: 8 (over y, core).
Axes of the slice: x: 4, y: 4, z: 4, core: 2. Of those that a mesh axis runs over, the one named last changes fastest.
Arguments:
- frames: bfloat16 [4096, 1536], P('dp', 'tensor'), may hold values from -6 to 6
- counts: int32 [16], P('dp'), may hold values from 1 to 256, as said below
- layer_norm_gain1: float32 [1536], replicated, may hold values from 0.1 to 1.9
- w_in: bfloat16 [1536, 4096], P('dp', 'tensor'), may hold values from -0.15625 to 0.15625
- w_out: bfloat16 [4096, 1536], P('tensor', 'dp'), may hold values from -0.09375 to 0.09375
- norm_gain2: float32 [1536], replicated, may hold values from 0.1 to 1.9
- w_adapt: bfloat16 [1536, 8192], P('dp', 'tensor'), may hold values from -0.15625 to 0.15625
- grad_out: bfloat16 [4096, 8192], P('dp', 'tensor'), may hold values from -0.1796875 to 0.1796875
Outputs:
- adapted: bfloat16 [4096, 8192], P('dp', 'tensor')
- frames_gradient: float32 [4096, 1536], P('dp', 'tensor')
- grad_in: float32 [1536, 4096], P('dp', 'tensor')
- grad_outw: float32 [4096, 1536], P('tensor', 'dp')
- grad_adapt: float32 [1536, 8192], P('dp', 'tensor')
- gain1_gradient: float32 [1536], replicated
- grad_gain2: float32 [1536], replicated
Inputs may be any that keep to these rules, and one draw needn't show every extreme that they name: `counts`: each utterance has 1 to 256 live frames; some utterance has all 256. Indices of dp differ in their typical lengths by up to four times.
All inputs are finite; a program needn't handle non-finite values.
Results may differ from a plain program's by a relative error of at most 0.006.
Values may be sent and summed in bfloat16 or wider, within the bound.
A program may use at most 128 MiB of HBM per device.

v0:
```python
import jax
import jax.numpy as jnp
from jax import lax
from jax.sharding import PartitionSpec as P

EPS = 1e-05


def apply_layer_norm(values):
    center = values - jnp.mean(values, axis=-1, keepdims=True)
    scale = lax.rsqrt(jnp.mean(center * center, axis=-1, keepdims=True) + EPS)
    return (center * scale, scale)


def norm_input_gradient(d_hat, vhat, scale):
    first = jnp.mean(d_hat, axis=-1, keepdims=True)
    second = jnp.mean(d_hat * vhat, axis=-1, keepdims=True)
    return scale * (d_hat - first - vhat * second)


def contract(left, right, left_dim, right_dim):
    return lax.dot_general(
        left, right, (((left_dim,), (right_dim,)), ((), ())), preferred_element_type=jnp.float32
    )


def on_device(frames, counts, layer_norm_gain1, w_in, w_out, norm_gain2, w_adapt, grad_out):
    slot_count = frames.shape[0]
    utt_count = counts.shape[0]
    span_len = slot_count // utt_count
    live = jnp.arange(span_len, dtype=jnp.int32)[None, :] < counts[:, None]
    live_mask = live.reshape(-1).astype(jnp.bfloat16)
    whole_in, whole_out, whole_adapt = (
        lax.all_gather(w_in, "dp", axis=0, tiled=True),
        lax.all_gather(w_out, "dp", axis=1, tiled=True),
        lax.all_gather(w_adapt, "dp", axis=0, tiled=True),
    )
    local_frames, local_cot, local_mask = (frames, grad_out, live_mask)
    full_frames = lax.all_gather(local_frames, "tensor", axis=1, tiled=True)
    width = full_frames.shape[1]
    hid_cols = whole_in.shape[1]
    out_cols = whole_adapt.shape[1]
    block = min(128, slot_count)
    acc_in = jnp.zeros((width, hid_cols), jnp.float32)
    acc_out = jnp.zeros((hid_cols, width), jnp.float32)
    acc_adapt = jnp.zeros((width, out_cols), jnp.float32)
    gain1_accumulator = jnp.zeros((width,), jnp.float32)
    acc_gain2 = jnp.zeros((width,), jnp.float32)
    adapted_parts = []
    gradient_pieces = []
    for step in range(slot_count // block):
        lower = step * block
        frames_per_block = full_frames[lower : lower + block].astype(jnp.float32)
        block_mask = local_mask[lower : lower + block]
        block_cot = local_cot[lower : lower + block] * block_mask[:, None]
        is_live = jnp.any(block_mask > 0)
        normalized_input, inverse_deviation1 = apply_layer_norm(frames_per_block)
        hidden_activation = (normalized_input * layer_norm_gain1).astype(jnp.bfloat16)

        def front_work():
            pre_act = jnp.dot(hidden_activation, whole_in, preferred_element_type=jnp.float32)
            sig = jax.nn.sigmoid(pre_act)
            swished = (pre_act * sig).astype(jnp.bfloat16)
            return (
                pre_act,
                sig,
                swished,
                jnp.dot(swished, whole_out, preferred_element_type=jnp.float32),
            )

        def front_empty():
            zero_hid = jnp.zeros((block, hid_cols), jnp.float32)
            return (
                zero_hid,
                zero_hid,
                zero_hid.astype(jnp.bfloat16),
                jnp.zeros((block, width), jnp.float32),
            )

        pre_act, sig, swished, branch_part = lax.cond(is_live, front_work, front_empty)
        branch = lax.psum(branch_part, "tensor")
        resid = frames_per_block + 0.5 * branch
        yhat, rstd2 = apply_layer_norm(resid)
        normed = (yhat * norm_gain2).astype(jnp.bfloat16)

        def adapt_work():
            projected = jnp.dot(normed, whole_adapt, preferred_element_type=jnp.float32)
            return (
                projected * block_mask[:, None].astype(jnp.float32),
                contract(block_cot, whole_adapt, 1, 1),
            )

        def adapt_empty():
            return (
                jnp.zeros((block, out_cols), jnp.float32),
                jnp.zeros((block, width), jnp.float32),
            )

        projected, normed_part = lax.cond(is_live, adapt_work, adapt_empty)
        adapted_parts.append(projected.astype(jnp.bfloat16))
        d_normed = lax.psum(normed_part, "tensor")

        def back_work(carry):
            sum_in, sum_out, sum_adapt, sum_gain2 = carry
            sum_adapt = sum_adapt + contract(normed, block_cot, 0, 0)
            sum_gain2 = sum_gain2 + jnp.sum(d_normed * yhat, axis=0)
            residual_gradient = norm_input_gradient(d_normed * norm_gain2, yhat, rstd2)
            d_branch = (0.5 * residual_gradient).astype(jnp.bfloat16)
            sum_out = sum_out + contract(swished, d_branch, 0, 0)
            d_swished = contract(d_branch, whole_out, 1, 1)
            d_pre = (d_swished * sig * (1.0 + pre_act * (1.0 - sig))).astype(jnp.bfloat16)
            sum_in = sum_in + contract(hidden_activation, d_pre, 0, 0)
            return (
                (sum_in, sum_out, sum_adapt, sum_gain2),
                residual_gradient,
                contract(d_pre, whole_in, 1, 1),
            )

        def back_empty(carry):
            zero_rows = jnp.zeros((block, width), jnp.float32)
            return (carry, zero_rows, zero_rows)

        carried, residual_gradient, hidden_part = lax.cond(
            is_live, back_work, back_empty, (acc_in, acc_out, acc_adapt, acc_gain2)
        )
        acc_in, acc_out, acc_adapt, acc_gain2 = carried
        hidden_gradient = lax.psum(hidden_part, "tensor")
        gain1_accumulator = gain1_accumulator + jnp.sum(hidden_gradient * normalized_input, axis=0)
        gradient_pieces.append(
            residual_gradient
            + norm_input_gradient(
                hidden_gradient * layer_norm_gain1, normalized_input, inverse_deviation1
            )
        )
    adapted = jnp.concatenate(adapted_parts, axis=0)
    grad_full = jnp.concatenate(gradient_pieces, axis=0)
    own_width = frames.shape[1]
    frames_gradient = lax.dynamic_slice_in_dim(
        grad_full, lax.axis_index("tensor") * own_width, own_width, 1
    )
    grad_in, grad_adapt = (
        lax.psum_scatter(acc_in, "dp", scatter_dimension=0, tiled=True),
        lax.psum_scatter(acc_adapt, "dp", scatter_dimension=0, tiled=True),
    )
    grad_outw = lax.psum_scatter(acc_out, "dp", scatter_dimension=1, tiled=True)
    gain1_gradient, grad_gain2 = lax.psum((gain1_accumulator, acc_gain2), "dp")
    return (adapted, frames_gradient, grad_in, grad_outw, grad_adapt, gain1_gradient, grad_gain2)


def solution(mesh):
    return jax.shard_map(
        on_device,
        mesh=mesh,
        in_specs=(
            P("dp", "tensor"),
            P("dp"),
            P(),
            P("dp", "tensor"),
            P("tensor", "dp"),
            P(),
            P("dp", "tensor"),
            P("dp", "tensor"),
        ),
        out_specs=(
            P("dp", "tensor"),
            P("dp", "tensor"),
            P("dp", "tensor"),
            P("tensor", "dp"),
            P("dp", "tensor"),
            P(),
            P(),
        ),
        check_vma=False,
    )
```

profile of v0, /device:TPU:0, one launch (start us, length us, event | category | flops | bytes accessed | tf_op | source)
XLA Modules:
  0.0 726.4 jit_solution(18251900555294321164)
XLA Ops:
  10.6 14.2 %all_gather.13 = bf16[256,1536]{0,1:T(8,128)(2,1)S(1)} all-gather(bf16[256,192]{0,1:T(8,128)(2,1)} %param.20), channel_id=1, replica_groups=mesh['dp'=16,'tensor'=8] {'tensor'}, dimensions={1}, use_global_device_ids=true | all-gather | bytes 884736 | tf_op jit(solution)/shard_map/all_gather | solution.py:39
  27.0 29.7 %all-gather.6.cloned.1.call-done = bf16[1536,512]{1,0:T(8,128)(2,1)} async-done(((bf16[96,512]{1,0:T(8,128)(2,1)}), bf16[1536,512]{1,0:T(8,128)(2,1)}) %all-gather.6.cloned.1.call-update) | async-done | bytes 1572880 | tf_op jit(solution)/shard_map/all_gather | solution.py:34
  56.7 45.5 %all-gather.8.cloned.1.call-done = bf16[512,1536]{0,1:T(8,128)(2,1)} async-done(((bf16[512,96]{0,1:T(8,128)(2,1)}), bf16[512,1536]{0,1:T(8,128)(2,1)}) %all-gather.8.cloned.1.call-update) | async-done | bytes 1572880 | tf_op jit(solution)/shard_map/all_gather | solution.py:35
  102.3 4.4 conditional.6
  102.3 2.9 multiply_convert_fusion
  108.6 60.3 %all-reduce.8.cloned.1.call-done = f32[128,1536]{0,1:T(8,128)} async-done(((f32[128,1536]{0,1:T(8,128)}), f32[128,1536]{0,1:T(8,128)}) %all-reduce.8.cloned.1.call-update) | async-done | bytes 786448 | tf_op jit(solution)/shard_map/psum | solution.py:81
  171.4 4.8 conditional.8
  171.4 2.4 multiply_convert_fusion.1
  173.7 2.4 fusion.54
  176.2 2.4 copy.39
  181.2 57.9 %all-reduce.10.cloned.1.call-done = f32[128,1536]{0,1:T(8,128)} async-done(((f32[128,1536]{0,1:T(8,128)}), f32[128,1536]{0,1:T(8,128)}) %all-reduce.10.cloned.1.call-update) | async-done | bytes 786448 | tf_op jit(solution)/shard_map/psum | solution.py:81
  242.5 2.3 multiply_convert_fusion.9
  244.9 43.6 %all-gather.4.cloned.1.call-done = bf16[1536,1024]{1,0:T(8,128)(2,1)} async-done(((bf16[96,1024]{1,0:T(8,128)(2,1)}), bf16[1536,1024]{1,0:T(8,128)(2,1)}) %all-gather.4.cloned.1.call-update) | async-done | bytes 3145744 | tf_op jit(solution)/shard_map/all_gather | solution.py:36
  288.5 4.0 conditional.7
  288.5 3.3 fusion.48
  293.5 5.4 conditional.9
  293.5 4.1 fusion.49
  299.0 62.7 %all-reduce.14.cloned.1.call-done = (f32[128,1536]{1,0:T(8,128)}, f32[128,1536]{1,0:T(8,128)}) async-done(((f32[128,1536]{1,0:T(8,128)}, f32[128,1536]{1,0:T(8,128)}), (f32[128,1536]{1,0:T(8,128)}, f32[128,1536]{1,0:T(8,128)})) %all-reduce.14.cloned.1.call-update) | async-done | bytes 1572880 | tf_op jit(solution)/shard_map/psum | solution.py:101
  362.6 21.0 %conditional.10 = (f32[1536,512]{0,1:T(8,128)}, f32[512,1536]{0,1:T(8,128)}, f32[1536,1024]{1,0:T(8,128)}, f32[1536]{0:T(1024)}, f32[128,1536]{1,0:T(8,128)}, /*index=5*/f32[128,1536]{0,1:T(8,128)}) conditional(s32[]{:T(128)} %convert_element_type.70, () %tuple.68, (f32[128]{0:T(128)}, f32[128,1]{0,1:T(1,128)}, f32[128,1]{0,1:T(1,128)}, ...), branch_computations={%region_21.0_spmd, %region_22.26_spmd} | conditional | flops 1211300608 | bytes 36725352 | solution.py:123
  370.0 3.2 convolution_bitcast_fusion.1
  374.8 3.1 convolution_bitcast_fusion
  379.1 4.6 fusion.50
  383.7 25.1 %conditional.11 = (f32[1536,512]{0,1:T(8,128)}, f32[512,1536]{0,1:T(8,128)}, f32[1536,1024]{1,0:T(8,128)}, f32[1536]{0:T(1024)}, f32[128,1536]{1,0:T(8,128)}, /*index=5*/f32[128,1536]{0,1:T(8,128)}) conditional(s32[]{:T(128)} %convert_element_type.74, (f32[1536,512]{0,1:T(8,128)}, f32[512,1536]{0,1:T(8,128)}, f32[1536,1024]{1,0:T(8,128)}, ...), branch_computations={%region_30.0_spmd, %region_31.35_spmd} | conditional | flops 1214447872 | bytes 51954420 | solution.py:123
  389.9 4.3 fusion.10
  395.7 4.3 fusion.9
  402.4 6.4 convolution_add_fusion
  413.5 3.6 copy.53
  420.6 56.1 %all-reduce.12.cloned.1.call-done = (f32[128,1536]{0,1:T(8,128)}, f32[128,1536]{0,1:T(8,128)}) async-done(((f32[128,1536]{0,1:T(8,128)}, f32[128,1536]{0,1:T(8,128)}), (f32[128,1536]{0,1:T(8,128)}, f32[128,1536]{0,1:T(8,128)})) %all-reduce.12.cloned.1.call-update) | async-done | bytes 1572880 | tf_op jit(solution)/shard_map/psum | solution.py:127
  479.0 74.7 %all-reduce = (f32[1536]{0:T(1024)}, f32[1536]{0:T(1024)}) all-reduce(f32[1536]{0:T(1024)S(1)} %add.111, f32[1536]{0:T(1024)} %get-tuple-element.214), channel_id=1, replica_groups=mesh['dp'=16,'tensor'=8] {'dp'}, use_global_device_ids=true, to_apply=%region_43.0 | all-reduce | flops 3072 | bytes 24576 | tf_op jit(solution)/shard_map/psum | solution.py:146
  553.7 2.4 fusion.34
  556.8 78.3 %reduce-scatter.6.cloned.1.call-done = f32[512,96]{0,1:T(8,128)} async-done(((f32[512,1536]{0,1:T(8,128)}), f32[512,96]{0,1:T(8,128)}) %reduce-scatter.6.cloned.1.call-update) | async-done | bytes 196624 | tf_op jit(solution)/shard_map/reduce_scatter | solution.py:145
  635.1 84.4 %reduce-scatter.8.cloned.1.call-done = f32[96,1024]{1,0:T(8,128)} async-done(((f32[1536,1024]{1,0:T(8,128)}), f32[96,1024]{1,0:T(8,128)}) %reduce-scatter.8.cloned.1.call-update) | async-done | bytes 393232 | tf_op jit(solution)/shard_map/reduce_scatter | solution.py:143
  (150 shorter events, 50.7 us)
Async XLA Ops:
  7.2 49.6 %all-gather.6.cloned.1.call-start = ((), (), s32[]{:S(2)}) async-start(), calls=%async_computation.4 | async-start | bytes 1671168 | tf_op jit(solution)/shard_map/all_gather | solution.py:34
  7.9 94.4 %all-gather.8.cloned.1.call-start = ((), (), s32[]{:S(2)}) async-start(), calls=%async_computation.5 | async-start | bytes 1671168 | tf_op jit(solution)/shard_map/all_gather | solution.py:35
  8.6 160.3 %all-reduce.8.cloned.1.call-start = ((), (), s32[]{:S(2)}) async-start(), calls=%async_computation.6 | async-start | bytes 1572864 | tf_op jit(solution)/shard_map/psum | solution.py:81
  25.1 77.2 %copy-start.22 = (f32[128]{0:T(128)}, f32[128]{0:T(128)S(1)}, u32[]{:S(2)}) copy-start(f32[128]{0:T(128)S(1)} %broadcast_multiply_fusion.11) | copy-start | bytes 1540
  25.3 77.0 %copy-start.24 = (f32[128]{0:T(128)}, f32[128]{0:T(128)S(1)}, u32[]{:S(2)}) copy-start(f32[128]{0:T(128)S(1)} %add_rsqrt_fusion.3) | copy-start | bytes 1540
  106.7 63.6 %copy-start.19 = (f32[1536]{0:T(1024)S(1)}, f32[1536]{0:T(1024)}, u32[]{:S(2)}) copy-start(f32[1536]{0:T(1024)} %param.22) | copy-start | bytes 18436
  106.7 64.6 %copy-start.2 = (bf16[1536,512]{1,0:T(8,128)(2,1)S(1)}, bf16[1536,512]{1,0:T(8,128)(2,1)}, u32[]{:S(2)}) copy-start(bf16[1536,512]{1,0:T(8,128)(2,1)} %all-gather.6.cloned.1.call-done) | copy-start | bytes 4718596
  107.9 131.2 %all-reduce.10.cloned.1.call-start = ((), (), s32[]{:S(2)}) async-start(), calls=%async_computation.7 | async-start | bytes 1572864 | tf_op jit(solution)/shard_map/psum | solution.py:81
  108.6 62.7 %copy-start.20 = (f32[128]{0:T(128)}, f32[128]{0:T(128)S(1)}, u32[]{:S(2)}) copy-start(f32[128]{0:T(128)S(1)} %broadcast_multiply_fusion.9) | copy-start | bytes 1540
  176.2 62.9 %copy-start.9 = (f32[128,1536]{0,1:T(8,128)S(1)}, f32[128,1536]{0,1:T(8,128)}, u32[]{:S(2)}) copy-start(f32[128,1536]{0,1:T(8,128)} %all-reduce.8.cloned.1.call-done) | copy-start | bytes 2359300
  178.6 64.0 %copy-start.18 = (f32[1536]{0:T(1024)S(1)}, f32[1536]{0:T(1024)}, u32[]{:S(2)}) copy-start(f32[1536]{0:T(1024)} %param.25) | copy-start | bytes 18436
  178.6 109.9 %all-gather.4.cloned.1.call-start = ((), (), s32[]{:S(2)}) async-start(), calls=%async_computation.3 | async-start | bytes 3342336 | tf_op jit(solution)/shard_map/all_gather | solution.py:36
  179.2 182.5 %all-reduce.14.cloned.1.call-start = ((), (), s32[]{:S(2)}) async-start(), calls=%async_computation.12 | async-start | bytes 3145728 | tf_op jit(solution)/shard_map/psum | solution.py:101
  179.2 62.7 %copy-start.29 = (bf16[128]{0:T(256)(128)(2,1)}, bf16[128]{0:T(256)(128)(2,1)S(1)}, u32[]{:S(2)}) copy-start(bf16[128]{0:T(256)(128)(2,1)S(1)} %get-tuple-element.358) | copy-start | bytes 772
  179.3 62.7 %copy-start.31 = (bf16[128]{0:T(256)(128)(2,1)}, bf16[128]{0:T(256)(128)(2,1)S(1)}, u32[]{:S(2)}) copy-start(bf16[128]{0:T(256)(128)(2,1)S(1)} %get-tuple-element.357) | copy-start | bytes 772
  181.2 60.8 %copy-start.33 = (f32[128]{0:T(128)}, f32[128]{0:T(128)S(1)}, u32[]{:S(2)}) copy-start(f32[128]{0:T(128)S(1)} %broadcast_multiply_fusion.10) | copy-start | bytes 1540
  239.1 3.4 copy-start.10
  288.5 4.0 copy-start.11
  288.5 4.0 copy-start.14
  288.5 4.0 copy-start.30
  293.5 4.1 copy-start.1
  298.9 177.8 %all-reduce.12.cloned.1.call-start = ((), (), s32[]{:S(2)}) async-start(), calls=%async_computation.11 | async-start | bytes 3145728 | tf_op jit(solution)/shard_map/psum | solution.py:127
  364.1 4.6 copy-start.5
  395.7 6.7 copy-start.12
  395.7 6.7 copy-start.15
  413.4 143.4 %reduce-scatter.4.cloned.1.call-start = ((), (), s32[]{:S(2)}) async-start(), calls=%async_computation.8 | async-start | bytes 3342336 | tf_op jit(solution)/shard_map/reduce_scatter | solution.py:142
  417.1 218.0 %reduce-scatter.6.cloned.1.call-start = ((), (), s32[]{:S(2)}) async-start(), calls=%async_computation.9 | async-start | bytes 3342336 | tf_op jit(solution)/shard_map/reduce_scatter | solution.py:145
  417.8 301.7 %reduce-scatter.8.cloned.1.call-start = ((), (), s32[]{:S(2)}) async-start(), calls=%async_computation.10 | async-start | bytes 6684672 | tf_op jit(solution)/shard_map/reduce_scatter | solution.py:143
  417.9 58.8 %copy-start.21 = (f32[128]{0:T(128)S(1)}, f32[128]{0:T(128)}, u32[]{:S(2)}) copy-start(f32[128]{0:T(128)} %copy-done.20) | copy-start | bytes 1540
  417.9 58.8 %copy-start.23 = (f32[128]{0:T(128)S(1)}, f32[128]{0:T(128)}, u32[]{:S(2)}) copy-start(f32[128]{0:T(128)} %copy-done.22) | copy-start | bytes 1540
  417.9 58.8 %copy-start.25 = (f32[128]{0:T(128)S(1)}, f32[128]{0:T(128)}, u32[]{:S(2)}) copy-start(f32[128]{0:T(128)} %copy-done.24) | copy-start | bytes 1540
  417.9 58.8 %copy-start.27 = (f32[128]{0:T(128)S(1)}, f32[128]{0:T(128)}, u32[]{:S(2)}) copy-start(f32[128]{0:T(128)} %copy-done.26) | copy-start | bytes 1540
  (16 other events, 34.6 us)
Sparse Core Ops, SparseCore 0:
  10.2 46.5 all-gather.5
  58.9 43.3 all-gather.7
  108.0 60.8 all-reduce.7
  178.7 60.3 all-reduce.9
  241.1 47.2 all-gather.3
  299.1 62.5 all-reduce.13
  413.5 63.1 all-reduce.11
  480.6 75.3 reduce-scatter.3
  560.0 75.0 reduce-scatter.5
  639.0 80.5 reduce-scatter.7
where the time goes:
time: 727 us; the launch traced here: 726 us
  waiting for transfers between devices  522 us (72%)
  blocking collectives  88.9 us (12%)
  matrix products  50.3 us (7%)
  other arithmetic  28.5 us (4%)
  local copies, waits for them, and re-layouts  19.9 us (3%)
  between operations  16.4 us (2%)
    psum x2, waiting for transfers between devices, on_device(): branch = lax.psum(branch_part, 'tensor')  118 us
    reduce_scatter x1, waiting for transfers between devices, on_device(): lax.psum_scatter(acc_adapt, 'dp', scatter_dimension=0, tiled=True)  84.4 us
    reduce_scatter x1, waiting for transfers between devices, on_device(): grad_outw = lax.psum_scatter(acc_out, 'dp', scatter_dimension=1, tiled=True)  78.3 us
    psum x1, blocking collectives, on_device(): gain1_gradient, grad_gain2 = lax.psum((gain1_accumulator, acc_gain2), 'dp')  74.7 us
    psum x1, waiting for transfers between devices, on_device(): d_normed = lax.psum(normed_part, 'tensor')  62.7 us
    psum x1, waiting for transfers between devices, on_device(): hidden_gradient = lax.psum(hidden_part, 'tensor')  56.1 us
    all_gather x1, waiting for transfers between devices, on_device(): lax.all_gather(w_out, 'dp', axis=1, tiled=True)  45.5 us
    all_gather x1, waiting for transfers between devices, on_device(): lax.all_gather(w_adapt, 'dp', axis=0, tiled=True)  43.6 us
  transfers between devices with their start and end apart: 10, of which 9 were waited for; matrix products, arithmetic and copies ran while one was open for 3% of the time, Pallas kernels for 0%

commit v1 on v0

v1 whole, which is shorter than its diff:
```python
import functools

import jax
import jax.numpy as jnp
from jax import lax
from jax.experimental import pallas as pl
from jax.experimental.pallas import tpu as pltpu
from jax.sharding import PartitionSpec as P

EPS = 1e-05
BF = jnp.bfloat16
F32 = jnp.float32
MESH = pl.DeviceIdType.MESH
COPIES = 320


def wrap(value, size):
    return lax.rem(value + size, size)


class Place:
    def __init__(self):
        d, t = lax.axis_index("dp"), lax.axis_index("tensor")
        self.t = t
        self.at = {"x": d // 4, "z": d % 4, "y": t // 2, "c": t % 2}

    def shifted(self, axis, delta):
        return wrap(self.at[axis] + delta, 2 if axis == "c" else 4)

    def peer(self, axis, delta):
        if axis == "t":
            return {"tensor": wrap(self.t + delta, 8)}
        place = dict(self.at)
        place[axis] = self.shifted(axis, delta)
        if axis in ("x", "z"):
            return {"dp": place["x"] * 4 + place["z"]}
        return {"tensor": place["y"] * 2 + place["c"]}


class Net:
    def __init__(self, place, send, recv):
        self.place, self.send, self.recv = place, send, recv
        self.count = 0
        self.sent = []

    def copy(self, src, dst, axis, delta):
        number = self.count
        self.count += 1
        move = pltpu.make_async_remote_copy(
            src_ref=src,
            dst_ref=dst,
            send_sem=self.send.at[number],
            recv_sem=self.recv.at[number],
            device_id=self.place.peer(axis, delta),
            device_id_type=MESH,
        )
        move.start()
        self.sent.append(move)
        return number

    def arrived(self, number, ref):
        pltpu.make_async_remote_copy(
            src_ref=ref,
            dst_ref=ref,
            send_sem=self.send.at[number],
            recv_sem=self.recv.at[number],
            device_id=self.place.peer("c", 1),
            device_id_type=MESH,
        ).wait_recv()

    def drain(self):
        for move in self.sent:
            move.wait_send()


LOW, HIGH, ALL = pl.ds(0, 48), pl.ds(48, 48), slice(None)


class Gather:
    def __init__(self, net, src, buf, half, first, own, fine):
        self.net, self.src, self.buf, self.half, self.own, self.fine = net, src, buf, half, own, fine
        self.first, self.second = (first, "z" if first == "x" else "x")
        place = net.place
        self.p, self.q = place.at[self.first], place.at[self.second]

    def slot(self, i, j, rows=ALL):
        if self.first == "x":
            return self.buf.at[self.half, i, j, rows]
        return self.buf.at[self.half, j, i, rows]

    def ahead(self, delta):
        return self.net.place.shifted(self.first, delta)

    def across(self, delta):
        return self.net.place.shifted(self.second, delta)

    def both(self, src, dst, axis):
        return (self.net.copy(src, dst, axis, 1), self.net.copy(src, dst, axis, -1))

    def start(self):
        own = self.slot(self.p, self.q)
        self.one = self.both(self.src, own, self.first)
        self.waves = []
        if self.fine:
            self.waves.append((self.p, self.both(self.src, own, self.second)))

    def pass_on(self):
        net = self.net
        left, right = self.ahead(-1), self.ahead(1)
        net.arrived(self.one[0], self.slot(left, self.q))
        part = self.slot(left, self.q, LOW)
        low = net.copy(part, part, self.first, 1)
        net.arrived(self.one[1], self.slot(right, self.q))
        part = self.slot(right, self.q, HIGH)
        high = net.copy(part, part, self.first, -1)
        self.two = (low, high)
        if self.fine:
            for i in (left, right):
                self.wave(i)

    def wave(self, i):
        group = self.slot(i, self.q)
        self.waves.append((i, self.both(group, group, self.second)))

    def turn(self):
        far = self.ahead(2)
        self.net.arrived(self.two[0], self.slot(far, self.q, LOW))
        self.net.arrived(self.two[1], self.slot(far, self.q, HIGH))
        self.own.wait()
        self.wave(far if self.fine else ALL)

    def pass_across(self):
        net = self.net
        left, right = self.across(-1), self.across(1)
        self.last = []
        for i, numbers in self.waves:
            net.arrived(numbers[0], self.slot(i, left))
            part = self.slot(i, left, LOW)
            low = net.copy(part, part, self.second, 1)
            net.arrived(numbers[1], self.slot(i, right))
            part = self.slot(i, right, HIGH)
            high = net.copy(part, part, self.second, -1)
            self.last.append((i, low, high))

    def finish(self):
        far = self.across(2)
        for i, low, high in self.last:
            self.net.arrived(low, self.slot(i, far, LOW))
            self.net.arrived(high, self.slot(i, far, HIGH))


class Scatter:
    def __init__(self, net, buf, half, first, bufs, out, out_cols):
        self.net, self.buf, self.half = net, buf, half
        self.first, self.second = (first, "z" if first == "x" else "x")
        self.hop, self.near, self.total, self.hop2, self.near2 = bufs
        self.out, self.out_cols = out, out_cols

    def group(self, i, rows=ALL):
        if self.first == "x":
            return self.buf.at[self.half, i, :, rows]
        return self.buf.at[self.half, :, i, rows]

    def launch(self, block, hop, near, axis):
        net, place = self.net, self.net.place
        far, right, left = (place.shifted(axis, delta) for delta in (2, 1, -1))
        return (
            net.copy(block(far, LOW), hop(0), axis, 1),
            net.copy(block(far, HIGH), hop(1), axis, -1),
            net.copy(block(right, HIGH), near(0, HIGH), axis, 1),
            net.copy(block(left, LOW), near(1, LOW), axis, -1),
        )

    def relay(self, numbers, block, hop, near, axis):
        net, place = self.net, self.net.place
        right, left = place.shifted(axis, 1), place.shifted(axis, -1)
        net.arrived(numbers[0], hop(0))
        part = block(right, LOW)
        part[...] = (part[...].astype(F32) + hop(0)[...].astype(F32)).astype(BF)
        low = net.copy(part, near(0, LOW), axis, 1)
        net.arrived(numbers[1], hop(1))
        part = block(left, HIGH)
        part[...] = (part[...].astype(F32) + hop(1)[...].astype(F32)).astype(BF)
        high = net.copy(part, near(1, HIGH), axis, -1)
        return (low, high)

    def landed(self, numbers, more, near):
        net = self.net
        net.arrived(numbers[2], near(0, HIGH))
        net.arrived(more[0], near(0, LOW))
        net.arrived(numbers[3], near(1, LOW))
        net.arrived(more[1], near(1, HIGH))

    def hop_at(self, side):
        return self.hop.at[self.half, side]

    def near_at(self, side, rows=ALL):
        return self.near.at[self.half, side, :, rows]

    def total_at(self, j, rows=ALL):
        return self.total.at[self.half, j, rows]

    def hop2_at(self, side):
        return self.hop2.at[self.half, side]

    def near2_at(self, side, rows=ALL):
        return self.near2.at[self.half, side, rows]

    def start(self):
        self.one = self.launch(self.group, self.hop_at, self.near_at, self.first)

    def pass_on(self):
        self.two = self.relay(self.one, self.group, self.hop_at, self.near_at, self.first)

    def turn(self):
        self.landed(self.one, self.two, self.near_at)
        mine = self.group(self.net.place.at[self.first])
        total = mine[...].astype(F32) + self.near_at(0)[...].astype(F32) + self.near_at(1)[...].astype(F32)
        self.total[self.half] = total.astype(BF)
        self.three = self.launch(self.total_at, self.hop2_at, self.near2_at, self.second)

    def pass_across(self):
        self.four = self.relay(self.three, self.total_at, self.hop2_at, self.near2_at, self.second)

    def finish(self):
        self.landed(self.three, self.four, self.near2_at)
        mine = self.total_at(self.net.place.at[self.second])
        total = mine[...].astype(F32) + self.near2_at(0)[...].astype(F32) + self.near2_at(1)[...].astype(F32)
        self.out[:, self.out_cols] = total


class RowGather:
    def __init__(self, net, buf):
        self.net, self.buf = net, buf
        self.y, self.c = net.place.at["y"], net.place.at["c"]

    def start(self):
        net, own = self.net, self.buf.at[self.y, self.c]
        self.one = [(delta, net.copy(own, own, "y", delta)) for delta in (2, 1, -1)]
        self.side = [(self.y, net.copy(own, own, "c", 1))]

    def pass_on(self):
        net = self.net
        for delta, number in self.one[1:] + self.one[:1]:
            source = net.place.shifted("y", -delta)
            part = self.buf.at[source, self.c]
            net.arrived(number, part)
            self.side.append((source, net.copy(part, part, "c", 1)))

    def finish(self):
        other = 1 - self.c
        for source, number in self.side:
            self.net.arrived(number, self.buf.at[source, other])


class RowScatter:
    def __init__(self, net, part, side, sums, near):
        self.net, self.part, self.side, self.sums, self.near = net, part, side, sums, near
        self.y, self.c = net.place.at["y"], net.place.at["c"]

    def start(self):
        self.one = self.net.copy(self.part.at[:, 1 - self.c], self.side, "c", 1)

    def pair(self, row):
        return self.part[row, self.c].astype(F32) + self.side[row].astype(F32)

    def pass_on(self):
        net = self.net
        net.arrived(self.one, self.side)
        self.two = []
        for place, delta in enumerate((2, 1, -1)):
            self.sums[place] = self.pair(net.place.shifted("y", delta)).astype(BF)
            self.two.append(net.copy(self.sums.at[place], self.near.at[place], "y", delta))

    def finish(self):
        total = self.pair(self.y)
        for place, number in enumerate(self.two):
            self.net.arrived(number, self.near.at[place])
            total = total + self.near[place].astype(F32)
        return total


def row_norm(values):
    center = values - jnp.mean(values, axis=-1, keepdims=True)
    scale = lax.rsqrt(jnp.mean(center * center, axis=-1, keepdims=True) + EPS)
    return (center * scale, scale)


def row_norm_gradient(d_hat, vhat, scale):
    first = jnp.mean(d_hat, axis=-1, keepdims=True)
    second = jnp.mean(d_hat * vhat, axis=-1, keepdims=True)
    return scale * (d_hat - first - vhat * second)


def times(left, right):
    return jnp.dot(left, right, preferred_element_type=F32)


def times_t(left, right):
    return lax.dot_general(left, right, (((1,), (1,)), ((), ())), preferred_element_type=F32)


def kernel(
    frames, counts, gain1, gain2, w_in, w_out, w_ad, grad_out,
    adapted_o, fg_o, gin_o, gout_o, gad_o, gains_o,
    wi, wo, wa, gi, go, ga,
    hop_i, near_i, tot_i, hop2_i, near2_i,
    hop_o, near_o, tot_o, hop2_o, near2_o,
    hop_a, near_a, tot_a, hop2_a, near2_a,
    out_i, out_o, out_a,
    fr, rows, hid, nrm, dbr, across,
    part_b, side_b, sums_b, near_b,
    part_n, side_n, sums_n, near_n,
    part_h, side_h, sums_h, near_h,
    xhat, yhat, dres, cot, adapted, factor, swished, fgs, fgr,
    gn_c, gn_y, gn_x, gn_z, gn_out,
    send, recv, local,
):
    place = Place()
    net = Net(place, send, recv)
    x, z, y, c, t = place.at["x"], place.at["z"], place.at["y"], place.at["c"], place.t

    loads = []

    def load(src, dst):
        move = pltpu.make_async_copy(src, dst, local.at[len(loads)])
        move.start()
        loads.append(move)
        return move

    halves = {}
    for name, src, buf, width in (("i", w_in, wi, 256), ("o", w_out, wo, 256), ("a", w_ad, wa, 512)):
        for half in range(2):
            cut = src.at[:, pl.ds(half * width, width)]
            halves[name, half] = (cut, load(cut, buf.at[half, x, z]))
    cot_load = load(grad_out, cot)

    greeted = [("t", delta) for delta in range(1, 8)] + [(a, delta) for a in "xz" for delta in (1, -1, 2)]
    barrier = pltpu.get_barrier_semaphore()
    for axis, delta in greeted:
        pl.semaphore_signal(barrier, inc=1, device_id=place.peer(axis, delta), device_id_type=MESH)
    pl.semaphore_wait(barrier, len(greeted))

    frame_moves = [
        (delta, net.copy(frames.at[wrap(t + delta, 8)], fr.at[t], "t", delta)) for delta in range(1, 8)
    ]
    gathers = {}
    for name, buf in (("i", wi), ("o", wo), ("a", wa)):
        gathers[name] = []
        for half in range(2):
            src, own = halves[name, half]
            one = Gather(net, src, buf, half, "xz"[half], own, name == "i")
            one.start()
            gathers[name].append(one)

    def run(name, step):
        for one in gathers[name]:
            getattr(one, step)()

    fr[t] = frames[t]
    for delta, number in frame_moves:
        net.arrived(number, fr.at[wrap(t - delta, 8)])
    for piece in range(8):
        rows[:, piece * 192 : (piece + 1) * 192] = fr[piece].astype(F32)
    normal, rstd1 = row_norm(rows[...])
    xhat[...] = normal
    hid[y, c] = (normal * gain1[...]).astype(BF)
    hid_rows = RowGather(net, hid)
    hid_rows.start()

    run("i", "pass_on")
    run("o", "pass_on")
    run("i", "turn")
    run("o", "turn")

    cot_load.wait()
    live = lax.broadcasted_iota(jnp.int32, (256, 1), 0) < counts[0]
    cot[...] = jnp.where(live, cot[...].astype(F32), 0.0).astype(BF)

    run("i", "pass_across")
    hid_rows.pass_on()
    run("a", "pass_on")
    run("i", "finish")
    hid_rows.finish()

    def flat(ref):
        return ref[...].reshape(256, 1536)

    def front(half):
        pre = times(flat(hid), wi[half].reshape(1536, 256))
        sig = jax.nn.sigmoid(pre)
        swished[half] = (pre * sig).astype(BF)
        factor[half] = sig * (1.0 + pre * (1.0 - sig))

    front(0)
    front(1)
    run("a", "turn")
    run("o", "pass_across")
    run("o", "finish")

    def rows_out(part, left, weight):
        def body(i, carry):
            value = times_t(left(0), weight[0, i].reshape(384, -1))
            value = value + times_t(left(1), weight[1, i].reshape(384, -1))
            columns = pl.ds(pl.multiple_of(i * 384, 128), 384)
            part[:, :, :, columns] = value.astype(BF).reshape(4, 2, 32, 384)
            return carry

        lax.fori_loop(0, 4, body, 0)

    rows_out(part_b, lambda half: swished[half], wo)
    branch = RowScatter(net, part_b, side_b, sums_b, near_b)
    branch.start()
    branch.pass_on()
    run("a", "pass_across")

    resid = rows[...] + 0.5 * branch.finish()
    normal, rstd2 = row_norm(resid)
    yhat[...] = normal
    nrm[y, c] = (normal * gain2[...]).astype(BF)
    nrm_rows = RowGather(net, nrm)
    nrm_rows.start()

    run("a", "finish")
    rows_out(part_n, lambda half: cot[:, half * 512 : (half + 1) * 512], wa)
    d_norm = RowScatter(net, part_n, side_n, sums_n, near_n)
    d_norm.start()
    nrm_rows.pass_on()
    d_norm.pass_on()
    nrm_rows.finish()

    def outer(grad, half, right):
        def body(i, carry):
            left = across[pl.ds(pl.multiple_of(i * 384, 128), 384), :]
            grad[half, i] = times(left, right).astype(BF).reshape(4, 96, -1)
            return carry

        lax.fori_loop(0, 4, body, 0)

    def scatter(buf, bufs, out, width):
        return [
            Scatter(net, buf, half, "zx"[half], bufs, out, pl.ds(half * width, width)) for half in range(2)
        ]

    sc_a = scatter(ga, (hop_a, near_a, tot_a, hop2_a, near2_a), out_a, 512)
    sc_o = scatter(go, (hop_o, near_o, tot_o, hop2_o, near2_o), out_o, 256)
    sc_i = scatter(gi, (hop_i, near_i, tot_i, hop2_i, near2_i), out_i, 256)

    def step(ones, name):
        for one in ones:
            getattr(one, name)()

    across[...] = flat(nrm).T
    for half in range(2):
        outer(ga, half, cot[:, half * 512 : (half + 1) * 512])
        sc_a[half].start()

    for half in range(2):
        value = times(flat(nrm), wa[half].reshape(1536, 512))
        adapted[:, half * 512 : (half + 1) * 512] = jnp.where(live, value, 0.0).astype(BF)
    stores = [load(adapted, adapted_o)]

    d_normed = d_norm.finish()
    gain2_part = jnp.sum(d_normed * yhat[...], axis=0, keepdims=True)
    d_resid = row_norm_gradient(d_normed * gain2[...], yhat[...], rstd2)
    dres[...] = d_resid
    dbr[y, c] = (0.5 * d_resid).astype(BF)
    dbr_rows = RowGather(net, dbr)
    dbr_rows.start()
    step(sc_a, "pass_on")
    dbr_rows.pass_on()
    dbr_rows.finish()

    pres = []
    for half in range(2):
        d_swished = times(flat(dbr), wo[half].reshape(1536, 256))
        pres.append((d_swished * factor[half]).astype(BF))
    rows_out(part_h, lambda half: pres[half], wi)
    d_hid = RowScatter(net, part_h, side_h, sums_h, near_h)
    d_hid.start()
    across[...] = flat(dbr).T
    for half in range(2):
        outer(go, half, swished[half])
        sc_o[half].start()
    d_hid.pass_on()
    across[...] = flat(hid).T
    for half in range(2):
        outer(gi, half, pres[half])
        sc_i[half].start()
    step(sc_a, "turn")

    d_hidden = d_hid.finish()
    gn_c[c] = jnp.concatenate([jnp.sum(d_hidden * xhat[...], axis=0, keepdims=True), gain2_part], axis=0)
    gain_move = net.copy(gn_c.at[c], gn_c.at[c], "c", 1)
    grad_rows = dres[...] + row_norm_gradient(d_hidden * gain1[...], xhat[...], rstd1)
    for piece in range(8):
        fgs[piece] = grad_rows[:, piece * 192 : (piece + 1) * 192]
    fgr[t] = fgs[t]
    grad_moves = [
        (delta, net.copy(fgs.at[wrap(t + delta, 8)], fgr.at[t], "t", delta)) for delta in range(1, 8)
    ]

    net.arrived(gain_move, gn_c.at[1 - c])
    total = gn_c[0] + gn_c[1]

    def gain_start(buf, axis, total):
        own = place.at[axis]
        buf[own] = total
        return [(delta, net.copy(buf.at[own], buf.at[own], axis, delta)) for delta in (1, -1, 2)]

    def gain_sum(moves, buf, axis):
        for delta, number in moves:
            net.arrived(number, buf.at[place.shifted(axis, -delta)])
        return buf[0] + buf[1] + buf[2] + buf[3]

    moves = gain_start(gn_y, "y", total)
    step(sc_a, "pass_across")
    step(sc_o, "pass_on")
    total = gain_sum(moves, gn_y, "y")
    moves = gain_start(gn_x, "x", total)
    step(sc_i, "pass_on")
    total = gain_sum(moves, gn_x, "x")
    moves = gain_start(gn_z, "z", total)
    step(sc_a, "finish")
    stores.append(load(out_a, gad_o))
    step(sc_o, "turn")
    step(sc_i, "turn")
    for delta, number in grad_moves:
        net.arrived(number, fgr.at[wrap(t - delta, 8)])
    stores.append(load(fgr, fg_o))
    gn_out[...] = gain_sum(moves, gn_z, "z")
    stores.append(load(gn_out, gains_o))
    step(sc_o, "pass_across")
    step(sc_i, "pass_across")
    step(sc_o, "finish")
    stores.append(load(out_o, gout_o))
    step(sc_i, "finish")
    stores.append(load(out_i, gin_o))
    net.drain()
    for move in stores:
        move.wait()


def on_device(frames, counts, layer_norm_gain1, w_in, w_out, norm_gain2, w_adapt, grad_out):
    def weight(width):
        return pltpu.VMEM((2, 4, 4, 96, width), BF)

    def sums(width):
        return [
            pltpu.VMEM((2, 2, 4, 48, width), BF),
            pltpu.VMEM((2, 2, 4, 96, width), BF),
            pltpu.VMEM((2, 4, 96, width), BF),
            pltpu.VMEM((2, 2, 48, width), BF),
            pltpu.VMEM((2, 2, 96, width), BF),
        ]

    slots = pltpu.VMEM((4, 2, 32, 1536), BF)
    row_sums = [
        slots,
        pltpu.VMEM((4, 32, 1536), BF),
        pltpu.VMEM((3, 32, 1536), BF),
        pltpu.VMEM((3, 32, 1536), BF),
    ]
    scratch = (
        [weight(256), weight(256), weight(512)] * 2
        + sums(256)
        + sums(256)
        + sums(512)
        + [pltpu.VMEM((96, 512), F32), pltpu.VMEM((96, 512), F32), pltpu.VMEM((96, 1024), F32)]
        + [pltpu.VMEM((8, 32, 192), BF), pltpu.VMEM((32, 1536), F32)]
        + [slots] * 3
        + [pltpu.VMEM((1536, 256), BF)]
        + row_sums * 3
        + [pltpu.VMEM((32, 1536), F32)] * 3
        + [pltpu.VMEM((256, 1024), BF), pltpu.VMEM((256, 1024), BF)]
        + [pltpu.VMEM((2, 256, 256), F32), pltpu.VMEM((2, 256, 256), BF)]
        + [pltpu.VMEM((8, 32, 192), F32)] * 2
        + [pltpu.VMEM((2, 2, 1536), F32)]
        + [pltpu.VMEM((4, 2, 1536), F32)] * 3
        + [pltpu.VMEM((2, 1536), F32)]
        + [pltpu.SemaphoreType.DMA((COPIES,)), pltpu.SemaphoreType.DMA((COPIES,)), pltpu.SemaphoreType.DMA((16,))]
    )
    vmem, far = pl.BlockSpec(memory_space=pltpu.VMEM), pl.BlockSpec(memory_space=pl.ANY)
    shape = jax.ShapeDtypeStruct
    adapted, fg, gin, gout, gad, gains = pl.pallas_call(
        kernel,
        out_shape=(
            shape((256, 1024), BF),
            shape((8, 32, 192), F32),
            shape((96, 512), F32),
            shape((96, 512), F32),
            shape((96, 1024), F32),
            shape((2, 1536), F32),
        ),
        in_specs=[vmem, pl.BlockSpec(memory_space=pltpu.SMEM), vmem, vmem, far, far, far, far],
        out_specs=[far] * 6,
        scratch_shapes=scratch,
        compiler_params=pltpu.CompilerParams(
            collective_id=0, has_side_effects=True, vmem_limit_bytes=58 * 2**20
        ),
    )(
        frames.reshape(8, 32, 192),
        counts,
        layer_norm_gain1.reshape(1, 1536),
        norm_gain2.reshape(1, 1536),
        w_in,
        w_out.T,
        w_adapt,
        grad_out,
    )
    return (adapted, fg.reshape(256, 192), gin, gout.T, gad, gains[0], gains[1])


def solution(mesh):
    return jax.shard_map(
        on_device,
        mesh=mesh,
        in_specs=(
            P("dp", "tensor"),
            P("dp"),
            P(),
            P("dp", "tensor"),
            P("tensor", "dp"),
            P(),
            P("dp", "tensor"),
            P("dp", "tensor"),
        ),
        out_specs=(
            P("dp", "tensor"),
            P("dp", "tensor"),
            P("dp", "tensor"),
            P("tensor", "dp"),
            P("dp", "tensor"),
            P(),
            P(),
        ),
        check_vma=False,
    )
```

time: 727 us -> 119 us (0.16)
  waiting for transfers between devices: 522 us -> 0 us
  Pallas kernels: 0 us -> 108 us
  blocking collectives: 88.9 us -> 0 us
  matrix products: 50.3 us -> 0 us
  other arithmetic: 28.5 us -> 0 us
  between operations: 16.4 us -> 1.31 us
  local copies, waits for them, and re-layouts: 19.9 us -> 9.96 us
    psum x4 -> x0, waiting for transfers between devices: 237 us -> none  [the longest x2 118 us: on_device(): branch = lax.psum(branch_part, 'tensor')]
    reduce_scatter x3 -> x0, waiting for transfers between devices: 163 us -> none  [the longest x1 84.4 us: on_device(): lax.psum_scatter(acc_adapt, 'dp', scatter_dimension=0, tiled=True)]
    all_gather x3 -> x0, waiting for transfers between devices: 119 us -> none  [the longest x1 45.5 us: on_device(): lax.all_gather(w_out, 'dp', axis=1, tiled=True)]
    pallas_call x0 -> x1, Pallas kernels: none -> 108 us  [on_device(): pl.pallas_call(kernel, out_shape=(shape((256, 1024), BF), shape((8, 32, 1...]
    psum x1 -> x0, blocking collectives: 74.7 us -> none  [on_device(): gain1_gradient, grad_gain2 = lax.psum((gain1_accumulator, acc_gain2), 'dp')]
    dot_general x18 -> x0, matrix products: 50.3 us -> none  [the longest x12 39.1 us: contract(): lax.dot_general(left, right, (((left_dim,), (right_dim,)), ((), ())), pre...]
    all_gather x1 -> x0, blocking collectives: 14.2 us -> none  [on_device(): full_frames = lax.all_gather(local_frames, 'tensor', axis=1, tiled=True)]
    cond x35 -> x0, local copies, waits for them, and re-layouts: 14.1 us -> none  [the longest x5 10.5 us: on_device(): lax.cond(is_live, back_work, back_empty, (acc_in, acc_out, acc_adapt, acc...]
  transfers between devices with their start and end apart: 10 -> 0, of which waited for: 9 -> 0; matrix products, arithmetic and copies ran while one was open for 3% -> 0% of each run, Pallas kernels for 0% -> 0%
where the time goes in v1:
time: 119 us
  Pallas kernels  108 us (91%)
  local copies, waits for them, and re-layouts  9.96 us (8%)
  between operations  1.31 us (1%)
    pallas_call x1, Pallas kernels, on_device(): pl.pallas_call(kernel, out_shape=(shape((256, 1024), BF), shape((8, 32, 1...  108 us
    unnamed x16, local copies, waits for them, and re-layouts  7.44 us

profile of v1, /device:TPU:0, one launch (start us, length us, event | category | flops | bytes accessed | tf_op | source)
XLA Modules:
  0.0 119.0 jit_solution(12763049161041953167)
XLA Ops:
  1.3 0.0 copy-start.4
  1.3 1.3 %reshape.27.gain1 = f32[1,1536]{1,0:T(1,128)} reshape(f32[1536]{0:T(1024)} %param.10) | data formatting | bytes 12288 | tf_op jit(solution)/shard_map/reshape | solution.py:604
  2.6 0.0 copy-done.4
  2.6 0.6 reshape.28.gain2
  3.2 1.7 %copy.15 = bf16[256,192]{1,0:T(8,128)(2,1)} copy(bf16[256,192]{0,1:T(8,128)(2,1)} %param.8) | data formatting | bytes 196608 | tf_op args[0]
  4.8 107.7 %shard_map.135 = (bf16[256,1024]{1,0:T(8,128)(2,1)}, f32[8,32,192]{2,1,0:T(8,128)}, f32[96,512]{1,0:T(8,128)}, f32[96,512]{1,0:T(8,128)}, f32[96,1024]{1,0:T(8,128)}, /*index=5*/f32[2,1536]{1,0:T(2,128)}) custom-call(bf16[8,32,192]{2,1,0:T(8,128)(2,1)} %bitcast.4, s32[1]{0:T(128)S(6)} %copy.21.counts, f32[1,1536]{1,0:T(1,128)} %reshape.27.gain1, ...), custom_call_target="tpu_custom_call" | custom-call | tf_op jit(solution)/shard_map/pallas_call | solution.py:585
  112.6 0.0 copy-start.3
  112.6 1.7 %copy.16 = f32[256,192]{0,1:T(8,128)} copy(f32[256,192]{1,0:T(8,128)} %bitcast.5) | data formatting | bytes 393216
  114.3 0.0 copy-done.3
  114.3 0.6 slice_reduce_fusion
  115.0 0.0 copy-start.2
  115.0 0.0 copy-start.1
  115.0 1.9 %copy.22 = bf16[256,1024]{1,0:T(8,128)(2,1)} copy(bf16[256,1024]{1,0:T(8,128)(2,1)} %get-tuple-element.35) | data formatting | bytes 1048576
  116.9 0.0 copy-done.2
  116.9 0.0 copy-start
  116.9 0.7 copy.23
  117.6 0.0 copy-done.1
  117.6 0.7 copy.24
  118.3 0.0 copy-done
  118.3 0.7 copy.25
Async XLA Ops:
  1.3 1.3 %copy-start.4 = (f32[1536]{0:T(1024)S(1)}, f32[1536]{0:T(1024)}, u32[]{:S(2)}) copy-start(f32[1536]{0:T(1024)} %param.13) | copy-start | bytes 18436
  112.6 1.8 %copy-start.3 = (f32[2,1536]{1,0:T(2,128)S(1)}, f32[2,1536]{1,0:T(2,128)}, u32[]{:S(2)}) copy-start(f32[2,1536]{1,0:T(2,128)} %get-tuple-element.18) | copy-start | bytes 36868
  115.0 1.9 %copy-start.2 = (f32[96,512]{1,0:T(8,128)S(1)}, f32[96,512]{1,0:T(8,128)}, u32[]{:S(2)}) copy-start(f32[96,512]{1,0:T(8,128)} %get-tuple-element.37) | copy-start | bytes 589828
  115.0 2.6 %copy-start.1 = (f32[96,512]{1,0:T(8,128)S(1)}, f32[96,512]{1,0:T(8,128)}, u32[]{:S(2)}) copy-start(f32[96,512]{1,0:T(8,128)} %get-tuple-element.16) | copy-start | bytes 589828
  116.9 1.4 %copy-start = (f32[96,1024]{1,0:T(8,128)S(1)}, f32[96,1024]{1,0:T(8,128)}, u32[]{:S(2)}) copy-start(f32[96,1024]{1,0:T(8,128)} %get-tuple-element.39) | copy-start | bytes 1179652

commit v2 on v1

v2 whole, which is shorter than its diff:
```python
import functools

import jax
import jax.numpy as jnp
from jax import lax
from jax.experimental import pallas as pl
from jax.experimental.pallas import tpu as pltpu
from jax.sharding import PartitionSpec as P

EPS = 1e-05
BF = jnp.bfloat16
F32 = jnp.float32
MESH = pl.DeviceIdType.MESH
LANES = 116


def wrap(value, size):
    return lax.rem(value + size, size)


class Place:
    def __init__(self):
        d, t = lax.axis_index("dp"), lax.axis_index("tensor")
        self.t = t
        self.at = {"x": d // 4, "z": d % 4, "y": t // 2, "c": t % 2}

    def shifted(self, axis, delta):
        return wrap(self.at[axis] + delta, 2 if axis == "c" else 4)

    def peer(self, axis, delta):
        if axis == "t":
            return {"tensor": wrap(self.t + delta, 8)}
        place = dict(self.at)
        place[axis] = self.shifted(axis, delta)
        if axis in ("x", "z"):
            return {"dp": place["x"] * 4 + place["z"]}
        return {"tensor": place["y"] * 2 + place["c"]}


class Net:
    def __init__(self, place, sems):
        self.place, self.sems = place, sems
        self.lanes = 0
        self.sent = []

    def lane(self):
        self.lanes += 1
        return self.lanes - 1

    def out_lane(self, gauge):
        lane = self.lane()
        self.sent.append((lane, gauge))
        return lane

    def copy(self, src, dst, axis, delta, out, into):
        pltpu.make_async_remote_copy(
            src_ref=src,
            dst_ref=dst,
            send_sem=self.sems.at[out],
            recv_sem=self.sems.at[into],
            device_id=self.place.peer(axis, delta),
            device_id_type=MESH,
        ).start()

    def whole(self, lane, gauge):
        return pltpu.make_async_remote_copy(
            src_ref=gauge,
            dst_ref=gauge,
            send_sem=self.sems.at[lane],
            recv_sem=self.sems.at[lane],
            device_id=self.place.peer("c", 1),
            device_id_type=MESH,
        )

    def arrived(self, lane, gauge):
        self.whole(lane, gauge).wait_recv()

    def drain(self):
        for lane, gauge in self.sent:
            self.whole(lane, gauge).wait_send()


LOW, HIGH, ALL = pl.ds(0, 48), pl.ds(48, 48), slice(None)


class Gather:
    def __init__(self, net, src, buf, half, first, own):
        self.net, self.src, self.buf, self.half, self.own = net, src, buf, half, own
        self.first, self.second = (first, "z" if first == "x" else "x")
        place = net.place
        self.p, self.q = place.at[self.first], place.at[self.second]
        self.out = net.out_lane(buf.at[half, pl.ds(0, 15)])
        self.near, self.far, self.last = net.lane(), net.lane(), net.lane()
        self.waves = [net.lane() for _ in range(3)]

    def slot(self, i, j, rows=ALL):
        return self.buf.at[self.half, i * 4 + j if self.first == "x" else j * 4 + i, rows]

    def wait(self, lane, blocks):
        self.net.arrived(lane, self.buf.at[self.half, pl.ds(0, blocks)])

    def both(self, src, dst, axis, lane):
        for delta in (1, -1):
            self.net.copy(src, dst, axis, delta, self.out, lane)

    def relay(self, slot, axis, lane):
        left, right = self.net.place.shifted(axis, -1), self.net.place.shifted(axis, 1)
        self.net.copy(slot(left, LOW), slot(left, LOW), axis, 1, self.out, lane)
        self.net.copy(slot(right, HIGH), slot(right, HIGH), axis, -1, self.out, lane)

    def ahead(self, delta):
        return self.net.place.shifted(self.first, delta)

    def wave(self, i, lane):
        block = self.slot(i, self.q)
        self.both(block, block, self.second, lane)

    def start(self):
        own = self.slot(self.p, self.q)
        self.both(self.src, own, self.first, self.near)
        self.both(self.src, own, self.second, self.waves[0])

    def pass_on(self):
        self.wait(self.near, 2)
        self.relay(lambda i, rows: self.slot(i, self.q, rows), self.first, self.far)
        self.wave(self.ahead(-1), self.waves[1])
        self.wave(self.ahead(1), self.waves[1])

    def turn(self):
        self.wait(self.far, 1)
        self.wave(self.ahead(2), self.waves[2])

    def across(self, i):
        self.relay(lambda j, rows: self.slot(i, j, rows), self.second, self.last)

    def across_own(self):
        self.wait(self.waves[0], 2)
        self.across(self.p)

    def across_next(self):
        self.wait(self.waves[1], 4)
        self.across(self.ahead(-1))
        self.across(self.ahead(1))

    def across_far(self):
        self.wait(self.waves[2], 2)
        self.across(self.ahead(2))

    def finish(self):
        self.wait(self.last, 4)
        self.own.wait()


class Scatter:
    def __init__(self, net, buf, half, first, bufs, gauge, out, out_cols):
        self.net, self.buf, self.half = net, buf, half
        self.first, self.second = (first, "z" if first == "x" else "x")
        self.hop, self.near, self.total, self.hop2, self.near2 = bufs
        self.out, self.out_cols = out, out_cols
        self.sends = net.out_lane(gauge.at[half, pl.ds(0, 15)])
        self.lanes = [net.lane() for _ in range(4)]

    def group(self, i, rows=ALL):
        if self.first == "x":
            return self.buf.at[self.half, i, :, rows]
        return self.buf.at[self.half, :, i, rows]

    def launch(self, block, hop, near, axis, lanes):
        place = self.net.place
        far, right, left = (place.shifted(axis, delta) for delta in (2, 1, -1))
        self.net.copy(block(far, LOW), hop(0), axis, 1, self.sends, lanes[0])
        self.net.copy(block(far, HIGH), hop(1), axis, -1, self.sends, lanes[0])
        self.net.copy(block(right, HIGH), near(0, HIGH), axis, 1, self.sends, lanes[1])
        self.net.copy(block(left, LOW), near(1, LOW), axis, -1, self.sends, lanes[1])

    def relay(self, block, hop, near, axis, lanes):
        place = self.net.place
        right, left = place.shifted(axis, 1), place.shifted(axis, -1)
        for side, part, rows, delta in ((0, block(right, LOW), LOW, 1), (1, block(left, HIGH), HIGH, -1)):
            part[...] = (part[...].astype(F32) + hop(side)[...].astype(F32)).astype(BF)
            self.net.copy(part, near(side, rows), axis, delta, self.sends, lanes[1])

    def hop_at(self, side):
        return self.hop.at[self.half, side]

    def near_at(self, side, rows=ALL):
        return self.near.at[self.half, side, :, rows]

    def total_at(self, j, rows=ALL):
        return self.total.at[self.half, j, rows]

    def hop2_at(self, side):
        return self.hop2.at[self.half, side]

    def near2_at(self, side, rows=ALL):
        return self.near2.at[self.half, side, rows]

    def start(self):
        self.launch(self.group, self.hop_at, self.near_at, self.first, self.lanes[:2])

    def pass_on(self):
        self.net.arrived(self.lanes[0], self.hop.at[self.half])
        self.relay(self.group, self.hop_at, self.near_at, self.first, self.lanes[:2])

    def turn(self):
        self.net.arrived(self.lanes[1], self.near.at[self.half])
        mine = self.group(self.net.place.at[self.first])
        total = mine[...].astype(F32) + self.near_at(0)[...].astype(F32) + self.near_at(1)[...].astype(F32)
        self.total[self.half] = total.astype(BF)
        self.launch(self.total_at, self.hop2_at, self.near2_at, self.second, self.lanes[2:])

    def pass_across(self):
        self.net.arrived(self.lanes[2], self.hop2.at[self.half])
        self.relay(self.total_at, self.hop2_at, self.near2_at, self.second, self.lanes[2:])

    def finish(self):
        self.net.arrived(self.lanes[3], self.near2.at[self.half])
        mine = self.total_at(self.net.place.at[self.second])
        total = mine[...].astype(F32) + self.near2_at(0)[...].astype(F32) + self.near2_at(1)[...].astype(F32)
        self.out[:, self.out_cols] = total


class RowGather:
    def __init__(self, net, buf):
        self.net, self.buf = net, buf
        self.y, self.c = net.place.at["y"], net.place.at["c"]
        self.out = net.out_lane(buf.at[pl.ds(0, 7)])
        self.near, self.far, self.side = net.lane(), net.lane(), net.lane()

    def slot(self, delta):
        return self.buf.at[self.net.place.shifted("y", delta) * 2 + self.c]

    def beside(self, delta):
        self.net.copy(self.slot(delta), self.slot(delta), "c", 1, self.out, self.side)

    def start(self):
        for delta in (1, -1, 2):
            lane = self.far if delta == 2 else self.near
            self.net.copy(self.slot(0), self.slot(0), "y", delta, self.out, lane)
        self.beside(0)

    def pass_near(self):
        self.net.arrived(self.near, self.buf.at[pl.ds(0, 2)])
        self.beside(-1)
        self.beside(1)

    def pass_far(self):
        self.net.arrived(self.far, self.slot(2))
        self.beside(2)

    def finish(self):
        self.net.arrived(self.side, self.buf.at[pl.ds(0, 4)])


class RowScatter:
    def __init__(self, net, bufs):
        self.net = net
        self.part, self.side, self.sums, self.near = bufs
        self.y, self.c = net.place.at["y"], net.place.at["c"]
        self.beside, self.out = net.out_lane(self.side), net.out_lane(self.sums)
        self.one = [net.lane() for _ in range(2)]
        self.two = [net.lane() for _ in range(2)]

    def put(self, i, value):
        self.part[i] = value.reshape(4, 2, 32, 384)
        self.net.copy(self.part.at[i, :, 1 - self.c], self.side.at[i], "c", 1, self.beside, self.one[i // 2])

    def pair(self, i, row):
        return self.part[i, row, self.c] + self.side[i, row]

    def pass_on(self, piece):
        net = self.net
        net.arrived(self.one[piece], self.side.at[pl.ds(2 * piece, 2)])
        for place, delta in enumerate((1, -1, 2)):
            row = net.place.shifted("y", delta)
            for k in range(2):
                self.sums[piece, place, :, k * 384 : (k + 1) * 384] = self.pair(2 * piece + k, row).astype(BF)
            net.copy(
                self.sums.at[piece, place], self.near.at[piece, place], "y", delta, self.out, self.two[piece]
            )

    def finish(self):
        halves = []
        for piece in range(2):
            total = jnp.concatenate([self.pair(2 * piece, self.y), self.pair(2 * piece + 1, self.y)], axis=1)
            self.net.arrived(self.two[piece], self.near.at[piece])
            for place in range(3):
                total = total + self.near[piece, place].astype(F32)
            halves.append(total)
        return jnp.concatenate(halves, axis=1)


def row_norm(values):
    center = values - jnp.mean(values, axis=-1, keepdims=True)
    scale = lax.rsqrt(jnp.mean(center * center, axis=-1, keepdims=True) + EPS)
    return (center * scale, scale)


def row_norm_gradient(d_hat, vhat, scale):
    first = jnp.mean(d_hat, axis=-1, keepdims=True)
    second = jnp.mean(d_hat * vhat, axis=-1, keepdims=True)
    return scale * (d_hat - first - vhat * second)


def times(left, right):
    return jnp.dot(left, right, preferred_element_type=F32)


def times_t(left, right):
    return lax.dot_general(left, right, (((1,), (1,)), ((), ())), preferred_element_type=F32)


def kernel(
    frames_in, counts, gain1_in, gain2_in, w_in, w_out, w_ad, grad_out,
    adapted_o, fg_o, gin_o, gout_o, gad_o, gain1_o, gain2_o,
    wi, wo, wa, gi, go, ga,
    hop_i, near_i, tot_i, hop2_i, near2_i,
    hop_o, near_o, tot_o, hop2_o, near2_o,
    hop_a, near_a, tot_a, hop2_a, near2_a,
    out_i, out_o, out_a,
    frames, gain1_v, gain2_v, own, fg,
    fr, rows, hid, nrm, dbr, hid_t, nrm_t, dbr_t,
    part_b, side_b, sums_b, near_b,
    part_n, side_n, sums_n, near_n,
    part_h, side_h, sums_h, near_h,
    xhat, yhat, dres, cot, adapted, factor, swished, fgs, fgr,
    gn_c, gn_y, gn_x, gn_z, gn_1, gn_2,
    sems, local,
):
    place = Place()
    net = Net(place, sems)
    x, z, y, c, t = place.at["x"], place.at["z"], place.at["y"], place.at["c"], place.t

    greeted = [("t", delta) for delta in range(1, 8)] + [(a, delta) for a in "xz" for delta in (1, -1, 2)]
    barrier = pltpu.get_barrier_semaphore()
    for axis, delta in greeted:
        pl.semaphore_signal(barrier, inc=1, device_id=place.peer(axis, delta), device_id_type=MESH)

    loads = []

    def load(src, dst):
        move = pltpu.make_async_copy(src, dst, local.at[len(loads)])
        move.start()
        loads.append(move)
        return move

    frames_load = load(frames_in, frames)
    gain_loads = [load(gain1_in, gain1_v), load(gain2_in, gain2_v)]
    gathers = []
    for src, buf, width in ((w_in, wi, 256), (w_out, wo, 256), (w_ad, wa, 512)):
        for half in range(2):
            cut = src.at[:, pl.ds(half * width, width)]
            gathers.append(Gather(net, cut, buf, half, "xz"[half], load(cut, buf.at[half, x * 4 + z])))
    i0, i1, o0, o1, a0, a1 = gathers
    cot_load = load(grad_out, cot)
    frames_load.wait()
    own[...] = frames[...].T.reshape(8, 32, 192)
    pl.semaphore_wait(barrier, len(greeted))

    def to_peers(src, dst, out, into):
        for delta in range(1, 8):
            net.copy(src.at[wrap(t + delta, 8)], dst.at[t], "t", delta, out, into)

    frames_lane = net.lane()
    to_peers(own, fr, net.out_lane(own.at[pl.ds(0, 7)]), frames_lane)
    i0.start()
    i1.start()
    cot_load.wait()
    live = lax.broadcasted_iota(jnp.int32, (256, 1), 0) < counts[0]
    cot[...] = jnp.where(live, cot[...].astype(F32), 0.0).astype(BF)

    fr[t] = own[t]
    for one in gain_loads:
        one.wait()
    gain1, gain2 = gain1_v[...].reshape(1, 1536), gain2_v[...].reshape(1, 1536)
    net.arrived(frames_lane, fr.at[pl.ds(0, 7)])
    for piece in range(8):
        rows[:, piece * 192 : (piece + 1) * 192] = fr[piece].astype(F32)
    normal, rstd1 = row_norm(rows[...])
    xhat[...] = normal
    hid[t] = (normal * gain1).astype(BF)
    hid_rows = RowGather(net, hid)
    hid_rows.start()

    i0.pass_on()
    i0.across_own()
    o0.start()
    o1.start()
    i1.pass_on()
    i1.across_own()
    i0.turn()
    o0.pass_on()
    i0.across_next()
    o1.across_own()
    o0.across_own()
    hid_rows.pass_near()
    hid_rows.pass_far()
    i1.across_next()
    o1.pass_on()
    hid_rows.finish()
    i1.turn()

    def flat(ref):
        return ref[...].reshape(256, 1536)

    hid_t[...] = flat(hid).T
    o0.turn()
    i0.across_far()
    o0.across_next()
    o1.across_next()
    o1.turn()
    a0.start()
    i1.across_far()
    a1.start()
    o0.across_far()

    def front(half):
        pre = times(flat(hid), wi[half].reshape(1536, 256))
        sig = jax.nn.sigmoid(pre)
        swished[half] = (pre * sig).astype(BF)
        factor[half] = sig * (1.0 + pre * (1.0 - sig))

    i0.finish()
    front(0)
    o1.across_far()
    a0.across_own()
    a0.pass_on()
    i1.finish()
    front(1)
    a1.pass_on()
    o0.finish()
    a1.across_own()
    o1.finish()

    def rows_out(scatter, left, weight):
        for i in range(4):
            some = slice(4 * i, 4 * i + 4)
            value = times_t(left(0), weight[0, some].reshape(384, -1))
            value = value + times_t(left(1), weight[1, some].reshape(384, -1))
            scatter.put(i, value)

    branch = RowScatter(net, (part_b, side_b, sums_b, near_b))
    rows_out(branch, lambda half: swished[half], wo)
    a0.turn()
    branch.pass_on(0)
    branch.pass_on(1)
    a0.across_next()
    a1.turn()
    a1.across_next()
    a0.across_far()

    resid = rows[...] + 0.5 * branch.finish()
    normal, rstd2 = row_norm(resid)
    yhat[...] = normal
    nrm[t] = (normal * gain2).astype(BF)
    nrm_rows = RowGather(net, nrm)
    nrm_rows.start()

    a1.across_far()
    a0.finish()
    a1.finish()
    d_norm = RowScatter(net, (part_n, side_n, sums_n, near_n))
    rows_out(d_norm, lambda half: cot[:, half * 512 : (half + 1) * 512], wa)
    d_norm.pass_on(0)
    nrm_rows.pass_near()
    nrm_rows.pass_far()
    d_norm.pass_on(1)
    nrm_rows.finish()

    def outer(grad, half, left, right):
        def body(i, carry):
            some = left[pl.ds(pl.multiple_of(i * 384, 128), 384), :]
            grad[half, i] = times(some, right).astype(BF).reshape(4, 96, -1)
            return carry

        lax.fori_loop(0, 4, body, 0)

    def scatter(buf, bufs, gauge, out, width):
        return [
            Scatter(net, buf, half, "zx"[half], bufs, gauge, out, pl.ds(half * width, width))
            for half in range(2)
        ]

    sa0, sa1 = scatter(ga, (hop_a, near_a, tot_a, hop2_a, near2_a), wa, out_a, 512)
    so0, so1 = scatter(go, (hop_o, near_o, tot_o, hop2_o, near2_o), wo, out_o, 256)
    si0, si1 = scatter(gi, (hop_i, near_i, tot_i, hop2_i, near2_i), wi, out_i, 256)

    nrm_t[...] = flat(nrm).T
    outer(ga, 0, nrm_t, cot[:, :512])
    sa0.start()
    outer(ga, 1, nrm_t, cot[:, 512:])
    sa1.start()

    for half in range(2):
        value = times(flat(nrm), wa[half].reshape(1536, 512))
        adapted[:, half * 512 : (half + 1) * 512] = jnp.where(live, value, 0.0).astype(BF)
    stores = [load(adapted, adapted_o)]

    d_normed = d_norm.finish()
    gain2_part = jnp.sum(d_normed * yhat[...], axis=0, keepdims=True)
    d_resid = row_norm_gradient(d_normed * gain2, yhat[...], rstd2)
    dres[...] = d_resid
    dbr[t] = (0.5 * d_resid).astype(BF)
    dbr_rows = RowGather(net, dbr)
    dbr_rows.start()
    sa0.pass_on()
    sa1.pass_on()
    dbr_rows.pass_near()
    dbr_rows.pass_far()
    dbr_rows.finish()

    dbr_t[...] = flat(dbr).T
    outer(go, 0, dbr_t, swished[0])
    so0.start()
    outer(go, 1, dbr_t, swished[1])
    so1.start()
    pres = []
    for half in range(2):
        d_swished = times(flat(dbr), wo[half].reshape(1536, 256))
        pres.append((d_swished * factor[half]).astype(BF))
    outer(gi, 0, hid_t, pres[0])
    si0.start()
    outer(gi, 1, hid_t, pres[1])
    si1.start()
    d_hid = RowScatter(net, (part_h, side_h, sums_h, near_h))
    rows_out(d_hid, lambda half: pres[half], wi)
    sa0.turn()
    d_hid.pass_on(0)
    d_hid.pass_on(1)
    sa1.turn()
    so0.pass_on()
    so1.pass_on()
    si0.pass_on()
    si1.pass_on()
    sa1.pass_across()

    d_hidden = d_hid.finish()
    gn_c[c] = jnp.concatenate([jnp.sum(d_hidden * xhat[...], axis=0, keepdims=True), gain2_part], axis=0)
    lane = net.lane()
    net.copy(gn_c.at[c], gn_c.at[c], "c", 1, net.out_lane(gn_c.at[0]), lane)
    grad_rows = dres[...] + row_norm_gradient(d_hidden * gain1, xhat[...], rstd1)
    for piece in range(8):
        fgs[piece] = grad_rows[:, piece * 192 : (piece + 1) * 192]
    fgr[t] = fgs[t]
    rows_lane = net.lane()
    to_peers(fgs, fgr, net.out_lane(fgs.at[pl.ds(0, 7)]), rows_lane)
    net.arrived(lane, gn_c.at[1 - c])
    total = gn_c[0] + gn_c[1]

    def gain_start(buf, axis, total):
        here = buf.at[place.at[axis]]
        here[...] = total
        out, into = net.out_lane(buf.at[pl.ds(0, 3)]), net.lane()
        for delta in (1, -1, 2):
            net.copy(here, here, axis, delta, out, into)
        return into

    def gain_sum(into, buf):
        net.arrived(into, buf.at[pl.ds(0, 3)])
        return buf[0] + buf[1] + buf[2] + buf[3]

    lane = gain_start(gn_y, "y", total)
    sa0.pass_across()
    so0.turn()
    so1.turn()
    lane = gain_start(gn_x, "x", gain_sum(lane, gn_y))
    net.arrived(rows_lane, fgr.at[pl.ds(0, 7)])
    fg[...] = fgr[...].reshape(256, 192).T
    stores.append(load(fg, fg_o))
    si0.turn()
    si1.turn()
    lane = gain_start(gn_z, "z", gain_sum(lane, gn_x))
    sa0.finish()
    sa1.finish()
    stores.append(load(out_a, gad_o))
    so0.pass_across()
    so1.pass_across()
    si0.pass_across()
    si1.pass_across()
    so0.finish()
    so1.finish()
    stores.append(load(out_o, gout_o))
    total = gain_sum(lane, gn_z)
    gn_1[...] = total[0]
    gn_2[...] = total[1]
    stores.append(load(gn_1, gain1_o))
    stores.append(load(gn_2, gain2_o))
    si0.finish()
    si1.finish()
    stores.append(load(out_i, gin_o))
    net.drain()
    for move in stores:
        move.wait()


def hand_over(*refs):
    count = len(refs) // 3
    sems = refs[-1]
    moves = []
    for i in range(count):
        hold = refs[2 * count + i]
        moves.append(
            (
                pltpu.make_async_copy(refs[i], hold, sems.at[0, i]),
                pltpu.make_async_copy(hold, refs[count + i], sems.at[1, i]),
            )
        )
        moves[-1][0].start()
    for come, go in moves:
        come.wait()
        go.start()
    for come, go in moves:
        go.wait()


def on_device(frames, counts, layer_norm_gain1, w_in, w_out, norm_gain2, w_adapt, grad_out):
    def weight(width):
        return pltpu.VMEM((2, 16, 96, width), BF)

    def gradient(width):
        return pltpu.VMEM((2, 4, 4, 96, width), BF)

    def sums(width):
        return [
            pltpu.VMEM((2, 2, 4, 48, width), BF),
            pltpu.VMEM((2, 2, 4, 96, width), BF),
            pltpu.VMEM((2, 4, 96, width), BF),
            pltpu.VMEM((2, 2, 48, width), BF),
            pltpu.VMEM((2, 2, 96, width), BF),
        ]

    slots = pltpu.VMEM((8, 32, 1536), BF)
    row_sums = [
        pltpu.VMEM((4, 4, 2, 32, 384), F32),
        pltpu.VMEM((4, 4, 32, 384), F32),
        pltpu.VMEM((2, 3, 32, 768), BF),
        pltpu.VMEM((2, 3, 32, 768), BF),
    ]
    scratch = (
        [weight(256), weight(256), weight(512), gradient(256), gradient(256), gradient(512)]
        + sums(256)
        + sums(256)
        + sums(512)
        + [pltpu.VMEM((96, 512), F32), pltpu.VMEM((96, 512), F32), pltpu.VMEM((96, 1024), F32)]
        + [pltpu.VMEM((192, 256), BF), pltpu.VMEM((1536,), F32), pltpu.VMEM((1536,), F32)]
        + [pltpu.VMEM((8, 32, 192), BF), pltpu.VMEM((192, 256), F32)]
        + [pltpu.VMEM((8, 32, 192), BF), pltpu.VMEM((32, 1536), F32)]
        + [slots] * 3
        + [pltpu.VMEM((1536, 256), BF)] * 3
        + row_sums * 3
        + [pltpu.VMEM((32, 1536), F32)] * 3
        + [pltpu.VMEM((256, 1024), BF), pltpu.VMEM((256, 1024), BF)]
        + [pltpu.VMEM((2, 256, 256), F32), pltpu.VMEM((2, 256, 256), BF)]
        + [pltpu.VMEM((8, 32, 192), F32)] * 2
        + [pltpu.VMEM((2, 2, 1536), F32)]
        + [pltpu.VMEM((4, 2, 1536), F32)] * 3
        + [pltpu.VMEM((1536,), F32)] * 2
        + [pltpu.SemaphoreType.DMA((LANES,)), pltpu.SemaphoreType.DMA((17,))]
    )
    far = pl.BlockSpec(memory_space=pl.ANY)
    shape = jax.ShapeDtypeStruct
    shapes = (
        shape((256, 1024), BF),
        shape((192, 256), F32),
        shape((96, 512), F32),
        shape((96, 512), F32),
        shape((96, 1024), F32),
        shape((1536,), F32),
        shape((1536,), F32),
    )
    results = pl.pallas_call(
        kernel,
        out_shape=shapes,
        in_specs=[far, pl.BlockSpec(memory_space=pltpu.SMEM)] + [far] * 6,
        out_specs=[far] * 7,
        scratch_shapes=scratch,
        compiler_params=pltpu.CompilerParams(
            collective_id=0, has_side_effects=True, vmem_limit_bytes=58 * 2**20
        ),
    )(
        frames.T,
        counts,
        layer_norm_gain1,
        norm_gain2,
        w_in,
        w_out.T,
        w_adapt,
        grad_out,
    )
    results = pl.pallas_call(
        hand_over,
        out_shape=shapes,
        in_specs=[far] * 7,
        out_specs=[far] * 7,
        scratch_shapes=[pltpu.VMEM(one.shape, one.dtype) for one in shapes] + [pltpu.SemaphoreType.DMA((2, 7))],
        compiler_params=pltpu.CompilerParams(vmem_limit_bytes=58 * 2**20),
    )(*results)
    adapted, fg, gin, gout, *others = results
    return (adapted, fg.T, gin, gout.T, *others)


def solution(mesh):
    return jax.shard_map(
        on_device,
        mesh=mesh,
        in_specs=(
            P("dp", "tensor"),
            P("dp"),
            P(),
            P("dp", "tensor"),
            P("tensor", "dp"),
            P(),
            P("dp", "tensor"),
            P("dp", "tensor"),
        ),
        out_specs=(
            P("dp", "tensor"),
            P("dp", "tensor"),
            P("dp", "tensor"),
            P("tensor", "dp"),
            P("dp", "tensor"),
            P(),
            P(),
        ),
        check_vma=False,
    )
```

time: 119 us -> 97.1 us (0.82)
  Pallas kernels: 108 us -> 95.6 us
  local copies, waits for them, and re-layouts: 9.96 us -> 0 us
    pallas_call x1 -> x2, Pallas kernels: 108 us -> 95.6 us  [the longest x1 93.4 us: on_device(): pl.pallas_call(kernel, out_shape=shapes, in_specs=[far, pl.BlockSpec(memo...]
    unnamed x16 -> x0, local copies, waits for them, and re-layouts: 7.44 us -> none
    reshape x2 -> x0, local copies, waits for them, and re-layouts: 1.9 us -> none  [the longest x1 1.3 us: on_device(): layer_norm_gain1.reshape(1, 1536)]
where the time goes in v2:
time: 97.1 us; the launch traced here: 96.9 us
  Pallas kernels  95.6 us (98%)
  between operations  1.29 us (1%)
    pallas_call x1, Pallas kernels, on_device(): pl.pallas_call(kernel, out_shape=shapes, in_specs=[far, pl.BlockSpec(memo...  93.4 us
    pallas_call x1, Pallas kernels, on_device(): pl.pallas_call(hand_over, out_shape=shapes, in_specs=[far] * 7, out_specs...  2.28 us

profile of v2, /device:TPU:0, one launch (start us, length us, event | category | flops | bytes accessed | tf_op | source)
XLA Modules:
  0.0 96.9 jit_solution(748112774542215257)
XLA Ops:
  1.3 93.4 %shard_map.135 = (bf16[256,1024]{1,0:T(8,128)(2,1)}, f32[192,256]{1,0:T(8,128)}, f32[96,512]{1,0:T(8,128)}, f32[96,512]{1,0:T(8,128)}, f32[96,1024]{1,0:T(8,128)}, /*index=5*/f32[1536]{0:T(1024)}, f32[1536]{0:T(1024)}) custom-call(bf16[192,256]{1,0:T(8,128)(2,1)} %bitcast.4, s32[1]{0:T(128)S(6)} %copy.15.counts, f32[1536]{0:T(1024)} %gain1_in.1, ...), custom_call_target="tpu_custom_call" | custom-call | tf_op jit(solution)/shard_map/pallas_call | solution.py:671
  94.7 2.3 %shard_map.136 = (bf16[256,1024]{1,0:T(8,128)(2,1)}, f32[192,256]{1,0:T(8,128)}, f32[96,512]{1,0:T(8,128)}, f32[96,512]{1,0:T(8,128)}, f32[96,1024]{1,0:T(8,128)}, /*index=5*/f32[1536]{0:T(1024)}, f32[1536]{0:T(1024)}) custom-call(bf16[256,1024]{1,0:T(8,128)(2,1)} %get-tuple-element.21.refs_0_, f32[192,256]{1,0:T(8,128)} %get-tuple-element.22.refs_1_, ...), custom_call_target="tpu_custom_call" | custom-call | tf_op jit(solution)/shard_map/pallas_call | solution.py:690

commit v3 on v2

v3 whole, which is shorter than its diff:
```python
import functools

import jax
import jax.numpy as jnp
from jax import lax
from jax.experimental import pallas as pl
from jax.experimental.pallas import tpu as pltpu
from jax.sharding import PartitionSpec as P

EPS = 1e-05
BF = jnp.bfloat16
F32 = jnp.float32
MESH = pl.DeviceIdType.MESH
LANES = 130


def wrap(value, size):
    return lax.rem(value + size, size)


class Place:
    def __init__(self):
        d, t = lax.axis_index("dp"), lax.axis_index("tensor")
        self.t = t
        self.at = {"x": d // 4, "z": d % 4, "y": t // 2, "c": t % 2}

    def shifted(self, axis, delta):
        return wrap(self.at[axis] + delta, 2 if axis == "c" else 4)

    def peer(self, axis, delta):
        if axis == "t":
            return {"tensor": wrap(self.t + delta, 8)}
        place = dict(self.at)
        place[axis] = self.shifted(axis, delta)
        if axis in ("x", "z"):
            return {"dp": place["x"] * 4 + place["z"]}
        return {"tensor": place["y"] * 2 + place["c"]}


class Net:
    def __init__(self, place, sems):
        self.place, self.sems = place, sems
        self.lanes = 0
        self.sent = []

    def lane(self):
        self.lanes += 1
        return self.lanes - 1

    def out_lane(self, gauge):
        lane = self.lane()
        self.sent.append((lane, gauge))
        return lane

    def copy(self, src, dst, axis, delta, out, into):
        pltpu.make_async_remote_copy(
            src_ref=src,
            dst_ref=dst,
            send_sem=self.sems.at[out],
            recv_sem=self.sems.at[into],
            device_id=self.place.peer(axis, delta),
            device_id_type=MESH,
        ).start()

    def whole(self, lane, gauge):
        return pltpu.make_async_remote_copy(
            src_ref=gauge,
            dst_ref=gauge,
            send_sem=self.sems.at[lane],
            recv_sem=self.sems.at[lane],
            device_id=self.place.peer("c", 1),
            device_id_type=MESH,
        )

    def arrived(self, lane, gauge):
        self.whole(lane, gauge).wait_recv()

    def drain(self):
        for lane, gauge in self.sent:
            self.whole(lane, gauge).wait_send()


LOW, HIGH, ALL = pl.ds(0, 48), pl.ds(48, 48), slice(None)
HALVES = (slice(0, 16), slice(16, 32))


class Gather:
    def __init__(self, net, src, buf, half, first, own):
        self.net, self.src, self.buf, self.half, self.own = net, src, buf, half, own
        self.first, self.second = (first, "z" if first == "x" else "x")
        place = net.place
        self.p, self.q = place.at[self.first], place.at[self.second]
        self.out = net.out_lane(buf.at[half, pl.ds(0, 15)])
        self.near, self.far, self.last = net.lane(), net.lane(), net.lane()
        self.waves = [net.lane() for _ in range(3)]

    def slot(self, i, j, rows=ALL):
        return self.buf.at[self.half, i * 4 + j if self.first == "x" else j * 4 + i, rows]

    def wait(self, lane, blocks):
        self.net.arrived(lane, self.buf.at[self.half, pl.ds(0, blocks)])

    def both(self, src, dst, axis, lane):
        for delta in (1, -1):
            self.net.copy(src, dst, axis, delta, self.out, lane)

    def relay(self, slot, axis, lane):
        left, right = self.net.place.shifted(axis, -1), self.net.place.shifted(axis, 1)
        self.net.copy(slot(left, LOW), slot(left, LOW), axis, 1, self.out, lane)
        self.net.copy(slot(right, HIGH), slot(right, HIGH), axis, -1, self.out, lane)

    def ahead(self, delta):
        return self.net.place.shifted(self.first, delta)

    def wave(self, i, lane):
        block = self.slot(i, self.q)
        self.both(block, block, self.second, lane)

    def start(self):
        self.both(self.src, self.slot(self.p, self.q), self.first, self.near)

    def start_across(self):
        self.both(self.src, self.slot(self.p, self.q), self.second, self.waves[0])

    def pass_on(self):
        self.wait(self.near, 2)
        self.relay(lambda i, rows: self.slot(i, self.q, rows), self.first, self.far)
        self.wave(self.ahead(-1), self.waves[1])
        self.wave(self.ahead(1), self.waves[1])

    def turn(self):
        self.wait(self.far, 1)
        self.wave(self.ahead(2), self.waves[2])

    def across(self, i):
        self.relay(lambda j, rows: self.slot(i, j, rows), self.second, self.last)

    def across_own(self):
        self.wait(self.waves[0], 2)
        self.across(self.p)

    def across_next(self):
        self.wait(self.waves[1], 4)
        self.across(self.ahead(-1))
        self.across(self.ahead(1))

    def across_far(self):
        self.wait(self.waves[2], 2)
        self.across(self.ahead(2))

    def finish(self):
        self.wait(self.last, 4)
        self.own.wait()


class Scatter:
    def __init__(self, net, buf, half, first, bufs, gauge, out, out_cols):
        self.net, self.buf, self.half = net, buf, half
        self.first, self.second = (first, "z" if first == "x" else "x")
        self.hop, self.near, self.total, self.last = bufs
        self.out, self.out_cols = out, out_cols
        self.sends = net.out_lane(gauge.at[half, pl.ds(0, 15)])
        self.lanes = [net.lane() for _ in range(3)]

    def group(self, i, rows=ALL):
        if self.first == "x":
            return self.buf.at[self.half, i, :, rows]
        return self.buf.at[self.half, :, i, rows]

    def hop_at(self, side):
        return self.hop.at[self.half, side]

    def near_at(self, side, rows=ALL):
        return self.near.at[self.half, side, :, rows]

    def start(self):
        far, right, left = (self.net.place.shifted(self.first, delta) for delta in (2, 1, -1))
        for part, into, delta, lane in (
            (self.group(far, LOW), self.hop_at(0), 1, 0),
            (self.group(far, HIGH), self.hop_at(1), -1, 0),
            (self.group(right, HIGH), self.near_at(0, HIGH), 1, 1),
            (self.group(left, LOW), self.near_at(1, LOW), -1, 1),
        ):
            self.net.copy(part, into, self.first, delta, self.sends, self.lanes[lane])

    def pass_on(self):
        self.net.arrived(self.lanes[0], self.hop.at[self.half])
        right, left = self.net.place.shifted(self.first, 1), self.net.place.shifted(self.first, -1)
        for side, part, rows, delta in (
            (0, self.group(right, LOW), LOW, 1),
            (1, self.group(left, HIGH), HIGH, -1),
        ):
            part[...] = (part[...].astype(F32) + self.hop_at(side)[...].astype(F32)).astype(BF)
            self.net.copy(part, self.near_at(side, rows), self.first, delta, self.sends, self.lanes[1])

    def turn(self):
        self.net.arrived(self.lanes[1], self.near.at[self.half])
        mine = self.group(self.net.place.at[self.first])
        total = mine[...].astype(F32) + self.near_at(0)[...].astype(F32) + self.near_at(1)[...].astype(F32)
        self.total[self.half] = total.astype(BF)
        for place, delta in enumerate((2, 1, -1)):
            part = self.total.at[self.half, self.net.place.shifted(self.second, delta)]
            self.net.copy(part, self.last.at[self.half, place], self.second, delta, self.sends, self.lanes[2])

    def finish(self):
        self.net.arrived(self.lanes[2], self.last.at[self.half])
        total = self.total[self.half, self.net.place.at[self.second]].astype(F32)
        for place in range(3):
            total = total + self.last[self.half, place].astype(F32)
        self.out[:, self.out_cols] = total


class RowGather:
    def __init__(self, net, buf, rows):
        self.net, self.buf, self.rows = net, buf, rows
        self.c = net.place.at["c"]
        self.out = net.out_lane(self.slots(7))
        self.near, self.far, self.side = net.lane(), net.lane(), net.lane()

    def slots(self, count):
        return self.buf.at[pl.ds(0, count), self.rows]

    def slot(self, delta):
        return self.buf.at[self.net.place.shifted("y", delta) * 2 + self.c, self.rows]

    def beside(self, delta):
        self.net.copy(self.slot(delta), self.slot(delta), "c", 1, self.out, self.side)

    def start(self):
        for delta in (1, -1, 2):
            lane = self.far if delta == 2 else self.near
            self.net.copy(self.slot(0), self.slot(0), "y", delta, self.out, lane)
        self.beside(0)

    def pass_on(self):
        self.net.arrived(self.near, self.slots(2))
        self.beside(-1)
        self.beside(1)
        self.net.arrived(self.far, self.slot(2))
        self.beside(2)

    def finish(self):
        self.net.arrived(self.side, self.slots(4))


class RowScatter:
    def __init__(self, net, bufs):
        self.net = net
        self.part, self.side, self.sums, self.near = bufs
        self.y, self.c = net.place.at["y"], net.place.at["c"]
        self.beside, self.out = net.out_lane(self.side), net.out_lane(self.sums)
        self.one, self.two = net.lane(), [net.lane() for _ in range(2)]

    def put(self, i, value):
        self.part[i] = value.reshape(4, 2, 32, 384)
        self.net.copy(self.part.at[i, :, 1 - self.c], self.side.at[i], "c", 1, self.beside, self.one)

    def pair(self, piece, row):
        rows = HALVES[piece]
        return [self.part[i, row, self.c, rows] + self.side[i, row, rows] for i in range(4)]

    def pass_on(self):
        net = self.net
        net.arrived(self.one, self.side)
        for piece in range(2):
            for place, delta in enumerate((1, -1, 2)):
                for i, value in enumerate(self.pair(piece, net.place.shifted("y", delta))):
                    self.sums[piece, place, :, i * 384 : (i + 1) * 384] = value.astype(BF)
                net.copy(
                    self.sums.at[piece, place], self.near.at[piece, place], "y", delta, self.out, self.two[piece]
                )

    def finish(self, piece):
        total = jnp.concatenate(self.pair(piece, self.y), axis=1)
        self.net.arrived(self.two[piece], self.near.at[piece])
        for place in range(3):
            total = total + self.near[piece, place].astype(F32)
        return total


def row_norm(values):
    center = values - jnp.mean(values, axis=-1, keepdims=True)
    scale = lax.rsqrt(jnp.mean(center * center, axis=-1, keepdims=True) + EPS)
    return (center * scale, scale)


def row_norm_gradient(d_hat, vhat, scale):
    first = jnp.mean(d_hat, axis=-1, keepdims=True)
    second = jnp.mean(d_hat * vhat, axis=-1, keepdims=True)
    return scale * (d_hat - first - vhat * second)


def times(left, right):
    return jnp.dot(left, right, preferred_element_type=F32)


def times_t(left, right):
    return lax.dot_general(left, right, (((1,), (1,)), ((), ())), preferred_element_type=F32)


def kernel(
    frames_in, counts, gain1_in, gain2_in, w_in, w_out, w_ad, grad_out,
    adapted_h, fg_h, gin_h, gout_h, gad_h, gain1_h, gain2_h,
    wi, wo, wa, gi, go, ga,
    hop_i, near_i, tot_i, last_i,
    hop_o, near_o, tot_o, last_o,
    hop_a, near_a, tot_a, last_a,
    adapted_o, fg_o, gin_o, gout_o, gad_o, gain1_o, gain2_o,
    frames, gain1_v, gain2_v, own,
    fr, rows, hid, nrm, dbr, hid_t, nrm_t, dbr_t,
    part_b, side_b, sums_b, near_b,
    part_n, side_n, sums_n, near_n,
    part_h, side_h, sums_h, near_h,
    xhat, yhat, dres, cot, factor, swished, fgs, fgr,
    gn_c, gn_y, gn_x, gn_z,
    sems, local,
):
    place = Place()
    net = Net(place, sems)
    x, z, y, c, t = place.at["x"], place.at["z"], place.at["y"], place.at["c"], place.t

    greeted = [("t", delta) for delta in range(1, 8)] + [(a, delta) for a in "xz" for delta in (1, -1, 2)]
    barrier = pltpu.get_barrier_semaphore()
    for axis, delta in greeted:
        pl.semaphore_signal(barrier, inc=1, device_id=place.peer(axis, delta), device_id_type=MESH)

    loads = []

    def load(src, dst):
        move = pltpu.make_async_copy(src, dst, local.at[len(loads)])
        move.start()
        loads.append(move)
        return move

    frames_load = load(frames_in, frames)
    gain_loads = [load(gain1_in, gain1_v), load(gain2_in, gain2_v)]
    gathers = []
    for src, buf, width in ((w_in, wi, 256), (w_out, wo, 256), (w_ad, wa, 512)):
        for half in range(2):
            cut = src.at[:, pl.ds(half * width, width)]
            gathers.append(Gather(net, cut, buf, half, "xz"[half], load(cut, buf.at[half, x * 4 + z])))
    i0, i1, o0, o1, a0, a1 = gathers
    cot_load = load(grad_out, cot)
    frames_load.wait()
    own[...] = frames[...].T.reshape(8, 32, 192)
    pl.semaphore_wait(barrier, len(greeted))

    def to_peers(src, dst, out, into):
        for delta in range(1, 8):
            net.copy(src.at[wrap(t + delta, 8)], dst.at[t], "t", delta, out, into)

    frames_lane = net.lane()
    to_peers(own, fr, net.out_lane(own.at[pl.ds(0, 7)]), frames_lane)
    for one in (i0, i1):
        one.start()
        one.start_across()
    o0.start()
    o1.start()
    cot_load.wait()
    live = lax.broadcasted_iota(jnp.int32, (256, 1), 0) < counts[0]
    cot[...] = jnp.where(live, cot[...].astype(F32), 0.0).astype(BF)

    fr[t] = own[t]
    for one in gain_loads:
        one.wait()
    gain1, gain2 = gain1_v[...].reshape(1, 1536), gain2_v[...].reshape(1, 1536)
    net.arrived(frames_lane, fr.at[pl.ds(0, 7)])
    for piece in range(8):
        rows[:, piece * 192 : (piece + 1) * 192] = fr[piece].astype(F32)
    normal, rstd1 = row_norm(rows[...])
    xhat[...] = normal
    hid[t] = (normal * gain1).astype(BF)
    hid_rows = RowGather(net, hid, slice(0, 32))
    hid_rows.start()

    i0.pass_on()
    i0.across_own()
    i1.across_own()
    i1.pass_on()
    o0.start_across()
    o1.start_across()
    o0.pass_on()
    o1.pass_on()
    i0.turn()
    i0.across_next()
    i1.turn()
    i1.across_next()
    hid_rows.pass_on()
    o0.across_own()
    o1.across_own()
    o0.turn()
    hid_rows.finish()

    def flat(ref):
        return ref[...].reshape(256, 1536)

    hid_t[...] = flat(hid).T
    o0.across_next()
    o1.turn()
    o1.across_next()
    i0.across_far()
    i1.across_far()
    o0.across_far()
    o1.across_far()
    a1.start()
    a0.start()
    a1.start_across()

    def front(half):
        pre = times(flat(hid), wi[half].reshape(1536, 256))
        sig = jax.nn.sigmoid(pre)
        swished[half] = (pre * sig).astype(BF)
        factor[half] = sig * (1.0 + pre * (1.0 - sig))

    i0.finish()
    front(0)
    i1.finish()
    front(1)
    a0.start_across()
    o0.finish()
    o1.finish()

    def rows_out(scatter, left, weight, look=None):
        for i in range(4):
            some = slice(4 * i, 4 * i + 4)
            value = times_t(left(0), weight[0, some].reshape(384, -1))
            value = value + times_t(left(1), weight[1, some].reshape(384, -1))
            scatter.put(i, value)
            if look is not None:
                look(i, value)

    branch = RowScatter(net, (part_b, side_b, sums_b, near_b))
    rows_out(branch, lambda half: swished[half], wo)
    branch.pass_on()
    a1.pass_on()
    a0.pass_on()
    a0.across_own()
    a1.across_own()

    rstd2 = []
    nrm_rows = [RowGather(net, nrm, piece) for piece in HALVES]

    def middle(piece):
        half = HALVES[piece]
        normal, scale = row_norm(rows[half] + 0.5 * branch.finish(piece))
        rstd2.append(scale)
        yhat[half] = normal
        nrm[t, half] = (normal * gain2).astype(BF)
        nrm_rows[piece].start()

    middle(0)
    a1.turn()
    middle(1)
    a0.turn()
    a1.across_next()
    nrm_rows[0].pass_on()
    a0.across_next()
    nrm_rows[1].pass_on()
    a1.across_far()
    a0.across_far()
    nrm_rows[0].finish()
    nrm_rows[1].finish()

    def outer(grad, half, left, right):
        def body(i, carry):
            some = left[pl.ds(pl.multiple_of(i * 384, 128), 384), :]
            grad[half, i] = times(some, right).astype(BF).reshape(4, 96, -1)
            return carry

        lax.fori_loop(0, 4, body, 0)

    def scatter(buf, bufs, gauge, out, width):
        return [
            Scatter(net, buf, half, "zx"[half], bufs, gauge, out, pl.ds(half * width, width))
            for half in range(2)
        ]

    sa0, sa1 = scatter(ga, (hop_a, near_a, tot_a, last_a), wa, gad_o, 512)
    so0, so1 = scatter(go, (hop_o, near_o, tot_o, last_o), wo, gout_o, 256)
    si0, si1 = scatter(gi, (hop_i, near_i, tot_i, last_i), wi, gin_o, 256)

    nrm_t[...] = flat(nrm).T
    outer(ga, 0, nrm_t, cot[:, :512])
    sa0.start()
    outer(ga, 1, nrm_t, cot[:, 512:])
    sa1.start()

    a0.finish()
    a1.finish()
    d_norm = RowScatter(net, (part_n, side_n, sums_n, near_n))
    rows_out(d_norm, lambda half: cot[:, half * 512 : (half + 1) * 512], wa)

    def adapt(half):
        value = times(flat(nrm), wa[half].reshape(1536, 512))
        adapted_o[:, half * 512 : (half + 1) * 512] = jnp.where(live, value, 0.0).astype(BF)

    adapt(0)
    d_norm.pass_on()
    adapt(1)
    stores = [load(adapted_o, adapted_h)]
    sa0.pass_on()
    sa1.pass_on()

    gain2_parts = []
    dbr_rows = [RowGather(net, dbr, piece) for piece in HALVES]

    def back(piece):
        half = HALVES[piece]
        d_normed, normal = d_norm.finish(piece), yhat[half]
        gain2_parts.append(jnp.sum(d_normed * normal, axis=0, keepdims=True))
        d_resid = row_norm_gradient(d_normed * gain2, normal, rstd2[piece])
        dres[half] = d_resid
        dbr[t, half] = (0.5 * d_resid).astype(BF)
        dbr_rows[piece].start()

    back(0)
    back(1)
    dbr_rows[0].pass_on()
    sa0.turn()
    dbr_rows[0].finish()
    dbr_rows[1].pass_on()
    sa1.turn()
    dbr_rows[1].finish()

    pres = []

    def before(half):
        d_swished = times(flat(dbr), wo[half].reshape(1536, 256))
        pres.append((d_swished * factor[half]).astype(BF))

    def gain_start(buf, axis, total):
        here = buf.at[place.at[axis]]
        here[...] = total
        out, into = net.out_lane(buf.at[pl.ds(0, 3)]), net.lane()
        for delta in (1, -1, 2):
            net.copy(here, here, axis, delta, out, into)
        return into

    def gain_sum(into, buf):
        net.arrived(into, buf.at[pl.ds(0, 3)])
        return buf[0] + buf[1] + buf[2] + buf[3]

    dbr_t[...] = flat(dbr).T
    outer(go, 0, dbr_t, swished[0])
    so0.start()
    outer(go, 1, dbr_t, swished[1])
    so1.start()
    before(0)
    before(1)
    d_hid = RowScatter(net, (part_h, side_h, sums_h, near_h))
    gain1_sums = []

    def look(i, value):
        some = hid[:, :, i * 384 : (i + 1) * 384].reshape(256, 384).astype(F32)
        gain1_sums.append(jnp.sum(value * some, axis=0, keepdims=True))

    rows_out(d_hid, lambda half: pres[half], wi, look)
    gain1_part = jnp.concatenate(gain1_sums, axis=1) / gain1
    gn_c[c] = jnp.concatenate([gain1_part, gain2_parts[0] + gain2_parts[1]], axis=0)
    lane = net.lane()
    net.copy(gn_c.at[c], gn_c.at[c], "c", 1, net.out_lane(gn_c.at[0]), lane)

    outer(gi, 0, hid_t, pres[0])
    si0.start()
    d_hid.pass_on()
    outer(gi, 1, hid_t, pres[1])
    si1.start()
    net.arrived(lane, gn_c.at[1 - c])
    lane = gain_start(gn_y, "y", gn_c[0] + gn_c[1])
    so0.pass_on()
    so1.pass_on()
    lane = gain_start(gn_x, "x", gain_sum(lane, gn_y))
    si0.pass_on()
    si1.pass_on()

    d_hidden = jnp.concatenate([d_hid.finish(0), d_hid.finish(1)], axis=0)
    grad_rows = dres[...] + row_norm_gradient(d_hidden * gain1, xhat[...], rstd1)
    for piece in range(8):
        fgs[piece] = grad_rows[:, piece * 192 : (piece + 1) * 192]
    fgr[t] = fgs[t]
    rows_lane = net.lane()
    to_peers(fgs, fgr, net.out_lane(fgs.at[pl.ds(0, 7)]), rows_lane)
    sa1.finish()
    sa0.finish()
    stores.append(load(gad_o, gad_h))
    lane = gain_start(gn_z, "z", gain_sum(lane, gn_x))
    so0.turn()
    so1.turn()
    net.arrived(rows_lane, fgr.at[pl.ds(0, 7)])
    fg_o[...] = fgr[...].reshape(256, 192).T
    stores.append(load(fg_o, fg_h))
    si0.turn()
    si1.turn()
    total = gain_sum(lane, gn_z)
    gain1_o[...] = total[0]
    gain2_o[...] = total[1]
    stores.append(load(gain1_o, gain1_h))
    stores.append(load(gain2_o, gain2_h))
    so0.finish()
    so1.finish()
    stores.append(load(gout_o, gout_h))
    si0.finish()
    si1.finish()
    stores.append(load(gin_o, gin_h))
    net.drain()
    for move in stores:
        move.wait()


def hand_over(*refs):
    count = len(refs) // 3
    sems = refs[-1]
    moves = []
    for i in range(count):
        hold = refs[2 * count + i]
        moves.append(
            (
                pltpu.make_async_copy(refs[i], hold, sems.at[0, i]),
                pltpu.make_async_copy(hold, refs[count + i], sems.at[1, i]),
            )
        )
        moves[-1][0].start()
    for come, go in moves:
        come.wait()
        go.start()
    for come, go in moves:
        go.wait()


def on_device(frames, counts, layer_norm_gain1, w_in, w_out, norm_gain2, w_adapt, grad_out):
    def weight(width):
        return pltpu.VMEM((2, 16, 96, width), BF)

    def gradient(width):
        return pltpu.VMEM((2, 4, 4, 96, width), BF)

    def sums(width):
        return [
            pltpu.VMEM((2, 2, 4, 48, width), BF),
            pltpu.VMEM((2, 2, 4, 96, width), BF),
            pltpu.VMEM((2, 4, 96, width), BF),
            pltpu.VMEM((2, 3, 96, width), BF),
        ]

    shape = jax.ShapeDtypeStruct
    shapes = (
        shape((256, 1024), BF),
        shape((192, 256), F32),
        shape((96, 512), F32),
        shape((96, 512), F32),
        shape((96, 1024), F32),
        shape((1536,), F32),
        shape((1536,), F32),
    )
    slots = pltpu.VMEM((8, 32, 1536), BF)
    row_sums = [
        pltpu.VMEM((4, 4, 2, 32, 384), F32),
        pltpu.VMEM((4, 4, 32, 384), F32),
        pltpu.VMEM((2, 3, 16, 1536), BF),
        pltpu.VMEM((2, 3, 16, 1536), BF),
    ]
    scratch = (
        [weight(256), weight(256), weight(512), gradient(256), gradient(256), gradient(512)]
        + sums(256)
        + sums(256)
        + sums(512)
        + [pltpu.VMEM(one.shape, one.dtype) for one in shapes]
        + [pltpu.VMEM((192, 256), BF), pltpu.VMEM((1536,), F32), pltpu.VMEM((1536,), F32)]
        + [pltpu.VMEM((8, 32, 192), BF)]
        + [pltpu.VMEM((8, 32, 192), BF), pltpu.VMEM((32, 1536), F32)]
        + [slots] * 3
        + [pltpu.VMEM((1536, 256), BF)] * 3
        + row_sums * 3
        + [pltpu.VMEM((32, 1536), F32)] * 3
        + [pltpu.VMEM((256, 1024), BF)]
        + [pltpu.VMEM((2, 256, 256), F32), pltpu.VMEM((2, 256, 256), BF)]
        + [pltpu.VMEM((8, 32, 192), F32)] * 2
        + [pltpu.VMEM((2, 2, 1536), F32)]
        + [pltpu.VMEM((4, 2, 1536), F32)] * 3
        + [pltpu.SemaphoreType.DMA((LANES,)), pltpu.SemaphoreType.DMA((17,))]
    )
    far = pl.BlockSpec(memory_space=pl.ANY)
    results = pl.pallas_call(
        kernel,
        out_shape=shapes,
        in_specs=[far, pl.BlockSpec(memory_space=pltpu.SMEM)] + [far] * 6,
        out_specs=[far] * 7,
        scratch_shapes=scratch,
        compiler_params=pltpu.CompilerParams(
            collective_id=0, has_side_effects=True, vmem_limit_bytes=58 * 2**20
        ),
    )(
        frames.T,
        counts,
        layer_norm_gain1,
        norm_gain2,
        w_in,
        w_out.T,
        w_adapt,
        grad_out,
    )
    results = pl.pallas_call(
        hand_over,
        out_shape=shapes,
        in_specs=[far] * 7,
        out_specs=[far] * 7,
        scratch_shapes=[pltpu.VMEM(one.shape, one.dtype) for one in shapes] + [pltpu.SemaphoreType.DMA((2, 7))],
        compiler_params=pltpu.CompilerParams(vmem_limit_bytes=58 * 2**20),
    )(*results)
    adapted, fg, gin, gout, *others = results
    return (adapted, fg.T, gin, gout.T, *others)


def solution(mesh):
    return jax.shard_map(
        on_device,
        mesh=mesh,
        in_specs=(
            P("dp", "tensor"),
            P("dp"),
            P(),
            P("dp", "tensor"),
            P("tensor", "dp"),
            P(),
            P("dp", "tensor"),
            P("dp", "tensor"),
        ),
        out_specs=(
            P("dp", "tensor"),
            P("dp", "tensor"),
            P("dp", "tensor"),
            P("tensor", "dp"),
            P("dp", "tensor"),
            P(),
            P(),
        ),
        check_vma=False,
    )
```

time: 97.1 us -> 92.1 us (0.949)
  Pallas kernels: 95.6 us -> 90.3 us
    pallas_call x1, Pallas kernels: 93.4 us -> 88 us  [on_device(): pl.pallas_call(kernel, out_shape=shapes, in_specs=[far, pl.BlockSpec(memo...]
where the time goes in v3:
time: 92.1 us; the launch traced here: 91.5 us
  Pallas kernels  90.3 us (98%)
  between operations  1.29 us (1%)
    pallas_call x1, Pallas kernels, on_device(): pl.pallas_call(kernel, out_shape=shapes, in_specs=[far, pl.BlockSpec(memo...  88 us
    pallas_call x1, Pallas kernels, on_device(): pl.pallas_call(hand_over, out_shape=shapes, in_specs=[far] * 7, out_specs...  2.28 us

profile of v3, /device:TPU:0, one launch (start us, length us, event | category | flops | bytes accessed | tf_op | source)
XLA Modules:
  0.0 91.5 jit_solution(11757607693021299705)
XLA Ops:
  1.3 88.0 %shard_map.135 = (bf16[256,1024]{1,0:T(8,128)(2,1)}, f32[192,256]{1,0:T(8,128)}, f32[96,512]{1,0:T(8,128)}, f32[96,512]{1,0:T(8,128)}, f32[96,1024]{1,0:T(8,128)}, /*index=5*/f32[1536]{0:T(1024)}, f32[1536]{0:T(1024)}) custom-call(bf16[192,256]{1,0:T(8,128)(2,1)} %bitcast.4, s32[1]{0:T(128)S(6)} %copy.15.counts, f32[1536]{0:T(1024)} %gain1_in.1, ...), custom_call_target="tpu_custom_call" | custom-call | tf_op jit(solution)/shard_map/pallas_call | solution.py:683
  89.3 2.3 %shard_map.136 = (bf16[256,1024]{1,0:T(8,128)(2,1)}, f32[192,256]{1,0:T(8,128)}, f32[96,512]{1,0:T(8,128)}, f32[96,512]{1,0:T(8,128)}, f32[96,1024]{1,0:T(8,128)}, /*index=5*/f32[1536]{0:T(1024)}, f32[1536]{0:T(1024)}) custom-call(bf16[256,1024]{1,0:T(8,128)(2,1)} %get-tuple-element.21.refs_0_, f32[192,256]{1,0:T(8,128)} %get-tuple-element.22.refs_1_, ...), custom_call_target="tpu_custom_call" | custom-call | tf_op jit(solution)/shard_map/pallas_call | solution.py:702

commit v4 on v3

--- a/solution.py
+++ b/solution.py
@@ -11,7 +11,7 @@
 BF = jnp.bfloat16
 F32 = jnp.float32
 MESH = pl.DeviceIdType.MESH
-LANES = 130
+LANES = 113
 
 
 def wrap(value, size):
@@ -299,14 +299,14 @@
 
 
 def kernel(
-    frames_in, counts, gain1_in, gain2_in, w_in, w_out, w_ad, grad_out,
+    frames_in, counts_in, gain1_in, gain2_in, w_in, w_out, w_ad, grad_out,
     adapted_h, fg_h, gin_h, gout_h, gad_h, gain1_h, gain2_h,
     wi, wo, wa, gi, go, ga,
     hop_i, near_i, tot_i, last_i,
     hop_o, near_o, tot_o, last_o,
     hop_a, near_a, tot_a, last_a,
     adapted_o, fg_o, gin_o, gout_o, gad_o, gain1_o, gain2_o,
-    frames, gain1_v, gain2_v, own,
+    counts, frames, gain1_v, gain2_v, own,
     fr, rows, hid, nrm, dbr, hid_t, nrm_t, dbr_t,
     part_b, side_b, sums_b, near_b,
     part_n, side_n, sums_n, near_n,
@@ -341,6 +341,7 @@
             gathers.append(Gather(net, cut, buf, half, "xz"[half], load(cut, buf.at[half, x * 4 + z])))
     i0, i1, o0, o1, a0, a1 = gathers
     cot_load = load(grad_out, cot)
+    counts_load = load(counts_in, counts)
     frames_load.wait()
     own[...] = frames[...].T.reshape(8, 32, 192)
     pl.semaphore_wait(barrier, len(greeted))
@@ -357,6 +358,7 @@
     o0.start()
     o1.start()
     cot_load.wait()
+    counts_load.wait()
     live = lax.broadcasted_iota(jnp.int32, (256, 1), 0) < counts[0]
     cot[...] = jnp.where(live, cot[...].astype(F32), 0.0).astype(BF)
 
@@ -665,7 +667,7 @@
         + sums(256)
         + sums(512)
         + [pltpu.VMEM(one.shape, one.dtype) for one in shapes]
-        + [pltpu.VMEM((192, 256), BF), pltpu.VMEM((1536,), F32), pltpu.VMEM((1536,), F32)]
+        + [pltpu.SMEM((1,), jnp.int32), pltpu.VMEM((192, 256), BF), pltpu.VMEM((1536,), F32), pltpu.VMEM((1536,), F32)]
         + [pltpu.VMEM((8, 32, 192), BF)]
         + [pltpu.VMEM((8, 32, 192), BF), pltpu.VMEM((32, 1536), F32)]
         + [slots] * 3
@@ -677,13 +679,13 @@
         + [pltpu.VMEM((8, 32, 192), F32)] * 2
         + [pltpu.VMEM((2, 2, 1536), F32)]
         + [pltpu.VMEM((4, 2, 1536), F32)] * 3
-        + [pltpu.SemaphoreType.DMA((LANES,)), pltpu.SemaphoreType.DMA((17,))]
+        + [pltpu.SemaphoreType.DMA((LANES,)), pltpu.SemaphoreType.DMA((18,))]
     )
     far = pl.BlockSpec(memory_space=pl.ANY)
     results = pl.pallas_call(
         kernel,
         out_shape=shapes,
-        in_specs=[far, pl.BlockSpec(memory_space=pltpu.SMEM)] + [far] * 6,
+        in_specs=[far] * 8,
         out_specs=[far] * 7,
         scratch_shapes=scratch,
         compiler_params=pltpu.CompilerParams(

time: 92.1 us -> 91.9 us (level)
  no operation moved by 1% of the time
where the time goes in v4:
time: 91.9 us; the launch traced here: 91.4 us
  Pallas kernels  90.1 us (98%)
  between operations  1.29 us (1%)
    pallas_call x1, Pallas kernels, on_device(): pl.pallas_call(kernel, out_shape=shapes, in_specs=[far] * 8, out_specs=[f...  87.8 us
    pallas_call x1, Pallas kernels, on_device(): pl.pallas_call(hand_over, out_shape=shapes, in_specs=[far] * 7, out_specs...  2.28 us

profile of v4, /device:TPU:0, one launch (start us, length us, event | category | flops | bytes accessed | tf_op | source)
XLA Modules:
  0.0 91.4 jit_solution(6861185534868145200)
XLA Ops:
  1.3 87.8 %shard_map.135 = (bf16[256,1024]{1,0:T(8,128)(2,1)}, f32[192,256]{1,0:T(8,128)}, f32[96,512]{1,0:T(8,128)}, f32[96,512]{1,0:T(8,128)}, f32[96,1024]{1,0:T(8,128)}, /*index=5*/f32[1536]{0:T(1024)}, f32[1536]{0:T(1024)}) custom-call(bf16[192,256]{1,0:T(8,128)(2,1)} %bitcast.4, s32[1]{0:T(128)S(6)} %copy.15.counts_in, f32[1536]{0:T(1024)} %gain1_in.1, ...), custom_call_target="tpu_custom_call" | custom-call | tf_op jit(solution)/shard_map/pallas_call | solution.py:685
  89.1 2.3 %shard_map.136 = (bf16[256,1024]{1,0:T(8,128)(2,1)}, f32[192,256]{1,0:T(8,128)}, f32[96,512]{1,0:T(8,128)}, f32[96,512]{1,0:T(8,128)}, f32[96,1024]{1,0:T(8,128)}, /*index=5*/f32[1536]{0:T(1024)}, f32[1536]{0:T(1024)}) custom-call(bf16[256,1024]{1,0:T(8,128)(2,1)} %get-tuple-element.21.refs_0_, f32[192,256]{1,0:T(8,128)} %get-tuple-element.22.refs_1_, ...), custom_call_target="tpu_custom_call" | custom-call | tf_op jit(solution)/shard_map/pallas_call | solution.py:704

commit v5 on v4

--- a/solution.py
+++ b/solution.py
@@ -227,17 +227,17 @@
         self.net.copy(self.slot(delta), self.slot(delta), "c", 1, self.out, self.side)
 
     def start(self):
-        for delta in (1, -1, 2):
+        for delta in (2, 1, -1):
             lane = self.far if delta == 2 else self.near
             self.net.copy(self.slot(0), self.slot(0), "y", delta, self.out, lane)
         self.beside(0)
 
     def pass_on(self):
+        self.net.arrived(self.far, self.slot(2))
+        self.beside(2)
         self.net.arrived(self.near, self.slots(2))
         self.beside(-1)
         self.beside(1)
-        self.net.arrived(self.far, self.slot(2))
-        self.beside(2)
 
     def finish(self):
         self.net.arrived(self.side, self.slots(4))
@@ -263,7 +263,7 @@
         net = self.net
         net.arrived(self.one, self.side)
         for piece in range(2):
-            for place, delta in enumerate((1, -1, 2)):
+            for place, delta in enumerate((2, 1, -1)):
                 for i, value in enumerate(self.pair(piece, net.place.shifted("y", delta))):
                     self.sums[piece, place, :, i * 384 : (i + 1) * 384] = value.astype(BF)
                 net.copy(

time: 91.9 us -> 91.8 us (level)
  no operation moved by 1% of the time
where the time goes in v5:
time: 91.8 us; the launch traced here: 90.8 us
  Pallas kernels  89.5 us (97%)
  between operations  1.29 us (1%)
    pallas_call x1, Pallas kernels, on_device(): pl.pallas_call(kernel, out_shape=shapes, in_specs=[far] * 8, out_specs=[f...  87.2 us
    pallas_call x1, Pallas kernels, on_device(): pl.pallas_call(hand_over, out_shape=shapes, in_specs=[far] * 7, out_specs...  2.28 us

profile of v5, /device:TPU:0, one launch (start us, length us, event | category | flops | bytes accessed | tf_op | source)
XLA Modules:
  0.0 90.8 jit_solution(7129655389760569974)
XLA Ops:
  1.3 87.2 %shard_map.135 = (bf16[256,1024]{1,0:T(8,128)(2,1)}, f32[192,256]{1,0:T(8,128)}, f32[96,512]{1,0:T(8,128)}, f32[96,512]{1,0:T(8,128)}, f32[96,1024]{1,0:T(8,128)}, /*index=5*/f32[1536]{0:T(1024)}, f32[1536]{0:T(1024)}) custom-call(bf16[192,256]{1,0:T(8,128)(2,1)} %bitcast.4, s32[1]{0:T(128)S(6)} %copy.15.counts_in, f32[1536]{0:T(1024)} %gain1_in.1, ...), custom_call_target="tpu_custom_call" | custom-call | tf_op jit(solution)/shard_map/pallas_call | solution.py:685
  88.5 2.3 %shard_map.136 = (bf16[256,1024]{1,0:T(8,128)(2,1)}, f32[192,256]{1,0:T(8,128)}, f32[96,512]{1,0:T(8,128)}, f32[96,512]{1,0:T(8,128)}, f32[96,1024]{1,0:T(8,128)}, /*index=5*/f32[1536]{0:T(1024)}, f32[1536]{0:T(1024)}) custom-call(bf16[256,1024]{1,0:T(8,128)(2,1)} %get-tuple-element.21.refs_0_, f32[192,256]{1,0:T(8,128)} %get-tuple-element.22.refs_1_, ...), custom_call_target="tpu_custom_call" | custom-call | tf_op jit(solution)/shard_map/pallas_call | solution.py:704
